TPU v7x, 32 devices: a whole 2x2x4 slice. The times are simulated.
32 devices in a mesh: groups: 2 (over x), slab: 16 (over z, y, core).
Axes of the slice: x: 2, y: 2, z: 4, core: 2. Of those that a mesh axis runs over, the one named last changes fastest.
Arguments:
- volume_features: bfloat16 [256, 32, 16, 384], P(('groups', 'slab')), parts along dimension 0, may hold values from -6 to 6
- focus_norm_factor: float32 [384], replicated, may hold values from 0.1 to 1.9
- perceptron_norm_factor: float32 [384], replicated, may hold values from 0.1 to 1.9
- courier_triple_projection: bfloat16 [384, 1152], replicated, may hold values from -24 to 24, as said below
- courier_result_projection: bfloat16 [384, 384], replicated, may hold values from -0.3125 to 0.3125
- region_triple_projection: bfloat16 [384, 1152], replicated, may hold values from -24 to 24, as said below
- region_result_projection: bfloat16 [384, 384], replicated, may hold values from -0.3125 to 0.3125
- perceptron_entry_projection: bfloat16 [384, 1536], replicated, may hold values from -0.3125 to 0.3125
- perceptron_exit_projection: bfloat16 [1536, 384], replicated, may hold values from -0.15625 to 0.15625
Outputs:
- result: bfloat16 [256, 32, 16, 384], P(('groups', 'slab')), parts along dimension 0
There are 2 independent parts, one for each index of `groups`. A program takes and returns all parts, laid end to end along the dimension named above; an argument that names none is the same for every part. Nothing has to cross between parts.
Inputs may be any that keep to these rules, and one draw needn't show every extreme that they name: `courier_triple_projection`: a projection for inputs of 384 features. `region_triple_projection`: a projection for inputs of 384 features.
All inputs are finite; a program needn't handle non-finite values.
Results may differ from a plain program's by a relative error of at most 0.0063.
Values may be sent and summed in bfloat16 or wider, within the bound.
A program may use at most 128 MiB of HBM per device.

v0:
```python
import jax
import jax.numpy as jnp
from jax import lax
from jax.sharding import PartitionSpec as P

EMBED_BREADTH = 384
FOCUS_BRANCHES = 12
BRANCH_BREADTH = 32
WIN = 8


def shifted_2(value, axis, steps):
    count = lax.axis_size(axis)
    pairs = [(source, (source + steps) % count) for source in range(count)]
    return lax.ppermute(value, axis, pairs)


def normalized_entries(values, gain):
    values = values.astype(jnp.float32)
    centre = jnp.mean(values, axis=-1, keepdims=True)
    shifted = values - centre
    spread = jnp.mean(shifted * shifted, axis=-1, keepdims=True)
    return shifted * lax.rsqrt(spread + 1e-05) * gain


def to_windows(scanned_solid, cubic_patch):
    planes, height, across, channels = scanned_solid.shape
    blocks = scanned_solid.reshape(
        planes // cubic_patch,
        cubic_patch,
        height // cubic_patch,
        cubic_patch,
        across // cubic_patch,
        cubic_patch,
        channels,
    )
    return blocks.transpose(0, 2, 4, 1, 3, 5, 6).reshape(-1, cubic_patch**3, channels)


def from_windows(windows, planes, height, across, cubic_patch):
    channels = windows.shape[-1]
    blocks = windows.reshape(
        planes // cubic_patch,
        height // cubic_patch,
        across // cubic_patch,
        cubic_patch,
        cubic_patch,
        cubic_patch,
        channels,
    )
    return blocks.transpose(0, 3, 1, 4, 2, 5, 6).reshape(planes, height, across, channels)


def window_local(stacked_entries, labels):
    count = stacked_entries.shape[0]
    similarity_multiplier = BRANCH_BREADTH ** (-0.5)
    asking_table = stacked_entries[:, :EMBED_BREADTH].reshape(count, FOCUS_BRANCHES, BRANCH_BREADTH)
    source_table = stacked_entries[:, EMBED_BREADTH : 2 * EMBED_BREADTH].reshape(
        count, FOCUS_BRANCHES, BRANCH_BREADTH
    )
    value_rows = stacked_entries[:, 2 * EMBED_BREADTH :].reshape(
        count, FOCUS_BRANCHES, BRANCH_BREADTH
    )
    similarity_table = (
        jnp.einsum("cfm,rfm->fcr", asking_table, source_table, preferred_element_type=jnp.float32)
        * similarity_multiplier
    )
    allowed = labels[:, None] == labels[None, :]
    ongoing_peak = jnp.max(jnp.where(allowed[None], similarity_table, -jnp.inf), axis=-1)
    weights = jnp.where(allowed[None], jnp.exp(similarity_table - ongoing_peak[..., None]), 0.0)
    ongoing_totals = jnp.sum(weights, axis=-1)
    interim_result = jnp.einsum(
        "tlq,qto->lto", weights.astype(jnp.bfloat16), value_rows, preferred_element_type=jnp.float32
    )
    return (interim_result, ongoing_totals, ongoing_peak)


def merge_courier(
    interim_result,
    ongoing_totals,
    ongoing_peak,
    stacked_entries,
    courier_lookup_entries,
    courier_content_entries,
):
    count = stacked_entries.shape[0]
    similarity_multiplier = BRANCH_BREADTH ** (-0.5)
    asking_table = (
        stacked_entries[:, :EMBED_BREADTH]
        .reshape(count, FOCUS_BRANCHES, BRANCH_BREADTH)
        .astype(jnp.float32)
    )
    courier_affinity = (
        jnp.sum(asking_table * courier_lookup_entries.astype(jnp.float32)[None], axis=-1)
        * similarity_multiplier
    )
    tile_peak = ongoing_peak.T
    tile_total = ongoing_totals.T
    ceiling_limit = jnp.maximum(tile_peak, courier_affinity)
    tile_correction = jnp.exp(tile_peak - ceiling_limit)
    courier_correction_factor = jnp.exp(courier_affinity - ceiling_limit)
    dividend_accumulator = (
        interim_result * tile_correction[..., None]
        + courier_correction_factor[..., None] * courier_content_entries.astype(jnp.float32)[None]
    )
    divisor_total = tile_total * tile_correction + courier_correction_factor
    return (
        (dividend_accumulator / divisor_total[..., None])
        .reshape(count, EMBED_BREADTH)
        .astype(jnp.bfloat16)
    )


def body(
    volume_features,
    focus_norm_factor,
    perceptron_norm_factor,
    courier_triple_projection,
    courier_result_projection,
    region_triple_projection,
    region_result_projection,
    perceptron_entry_projection,
    perceptron_exit_projection,
):
    devices = lax.axis_size("slab")
    position = lax.axis_index("slab")
    planes, height, across, channels = volume_features.shape
    half_window = WIN // 2
    similarity_multiplier = BRANCH_BREADTH ** (-0.5)
    arrived = shifted_2(volume_features[:half_window], "slab", -1)
    rolled = jnp.concatenate([volume_features[half_window:], arrived], axis=0)
    rolled = jnp.roll(rolled, (-half_window, -half_window), axis=(1, 2))
    plane_ids = position * planes + jnp.arange(planes, dtype=jnp.int32)
    z_label = (plane_ids >= devices * planes - half_window).astype(jnp.int32)
    y_label = (jnp.arange(height) >= height - half_window).astype(jnp.int32)
    x_label = (jnp.arange(across) >= across - half_window).astype(jnp.int32)
    labels = z_label[:, None, None] * 4 + y_label[None, :, None] * 2 + x_label[None, None, :]
    region_features = to_windows(rolled, WIN)
    region_identifiers = to_windows(labels[..., None], WIN)[..., 0]
    region_number = region_features.shape[0]
    courier_features = jnp.mean(region_features.astype(jnp.float32), axis=1)
    courier_normalized_entries = normalized_entries(courier_features, focus_norm_factor).astype(
        jnp.bfloat16
    )
    tok_normed = normalized_entries(region_features, focus_norm_factor).astype(jnp.bfloat16)
    stacked_entries = jnp.dot(
        tok_normed.reshape(-1, EMBED_BREADTH),
        region_triple_projection,
        preferred_element_type=jnp.float32,
    ).astype(jnp.bfloat16)
    stacked_entries = stacked_entries.reshape(region_number, WIN**3, 3 * EMBED_BREADTH)
    relay_asking_elements = jnp.dot(
        courier_normalized_entries,
        courier_triple_projection[:, :EMBED_BREADTH],
        preferred_element_type=jnp.float32,
    ).astype(jnp.bfloat16)
    relay_asking_elements = relay_asking_elements.reshape(
        region_number, FOCUS_BRANCHES, BRANCH_BREADTH
    )
    kv_local = jnp.dot(
        courier_normalized_entries,
        courier_triple_projection[:, EMBED_BREADTH:],
        preferred_element_type=jnp.float32,
    ).astype(jnp.bfloat16)
    piece = lax.all_gather(kv_local, "slab", axis=0, tiled=True)
    key_part = piece[:, :EMBED_BREADTH]
    old_peak = jnp.full((FOCUS_BRANCHES, region_number), -jnp.inf, jnp.float32)
    old_total = jnp.zeros((FOCUS_BRANCHES, region_number), jnp.float32)
    old_acc = jnp.zeros((FOCUS_BRANCHES, region_number, BRANCH_BREADTH), jnp.float32)
    rows = key_part.shape[0]
    source_table = key_part.reshape(rows, FOCUS_BRANCHES, BRANCH_BREADTH)
    value_rows = (
        piece[:, EMBED_BREADTH:].reshape(rows, FOCUS_BRANCHES, BRANCH_BREADTH).astype(jnp.float32)
    )
    similarity_table = (
        jnp.einsum(
            "cfm,rfm->fcr", relay_asking_elements, source_table, preferred_element_type=jnp.float32
        )
        * similarity_multiplier
    )
    new_peak = jnp.max(similarity_table, axis=-1)
    rescale = jnp.exp(old_peak - new_peak)
    softmax_weights_grid = jnp.exp(similarity_table - new_peak[..., None])
    new_total = old_total * rescale + jnp.sum(softmax_weights_grid, axis=-1)
    new_acc = old_acc * rescale[..., None] + jnp.einsum(
        "hqk,khd->hqd", softmax_weights_grid, value_rows, precision=lax.Precision.HIGHEST
    )
    courier_merge = (
        (new_acc / new_total[..., None])
        .transpose(1, 0, 2)
        .reshape(region_number, EMBED_BREADTH)
        .astype(jnp.bfloat16)
    )
    courier_delta_vector = jnp.dot(
        courier_merge, courier_result_projection, preferred_element_type=jnp.float32
    )
    revised_entries = courier_features + courier_delta_vector
    revised_normalized_entries = normalized_entries(revised_entries, focus_norm_factor).astype(
        jnp.bfloat16
    )
    courier_lookup_content = jnp.dot(
        revised_normalized_entries,
        region_triple_projection[:, EMBED_BREADTH:],
        preferred_element_type=jnp.float32,
    ).astype(jnp.bfloat16)
    courier_lookup_entries = courier_lookup_content[:, :EMBED_BREADTH].reshape(
        region_number, FOCUS_BRANCHES, BRANCH_BREADTH
    )
    courier_content_entries = courier_lookup_content[:, EMBED_BREADTH:].reshape(
        region_number, FOCUS_BRANCHES, BRANCH_BREADTH
    )
    courier_delta_vector, courier_lookup_entries, courier_content_entries = (
        courier_delta_vector,
        courier_lookup_entries,
        courier_content_entries,
    )

    def lone_region(region_members):
        interim_result, ongoing_totals, ongoing_peak = window_local(
            region_members[0], region_members[1]
        )
        return merge_courier(
            interim_result,
            ongoing_totals,
            ongoing_peak,
            region_members[0],
            region_members[2],
            region_members[3],
        )

    mixed_entries = lax.map(
        lone_region,
        (stacked_entries, region_identifiers, courier_lookup_entries, courier_content_entries),
    )
    mapped_entries = jnp.dot(
        mixed_entries.reshape(-1, EMBED_BREADTH),
        region_result_projection,
        preferred_element_type=jnp.float32,
    )
    mapped_entries = mapped_entries.reshape(region_number, WIN**3, EMBED_BREADTH)
    merged_entries = (
        region_features.astype(jnp.float32) + mapped_entries + courier_delta_vector[:, None, :]
    ).astype(jnp.bfloat16)
    flat = merged_entries.reshape(-1, EMBED_BREADTH)
    normed = normalized_entries(flat, perceptron_norm_factor).astype(jnp.bfloat16)
    hidden = jax.nn.gelu(
        jnp.dot(normed, perceptron_entry_projection, preferred_element_type=jnp.float32),
        approximate=True,
    ).astype(jnp.bfloat16)
    summed = flat.astype(jnp.float32) + jnp.dot(
        hidden, perceptron_exit_projection, preferred_element_type=jnp.float32
    )
    scanned_solid = from_windows(
        summed.astype(jnp.bfloat16).reshape(merged_entries.shape), planes, height, across, WIN
    )
    finished = jnp.roll(scanned_solid, (half_window, half_window), axis=(1, 2))
    returned = shifted_2(finished[half_window:], "slab", 1)
    return jnp.concatenate([returned, finished[:half_window]], axis=0)


def solution(mesh):
    placed = (P(("groups", "slab"), None, None, None), P(), P(), P(), P(), P(), P(), P(), P())
    return jax.shard_map(
        body,
        mesh=mesh,
        in_specs=placed,
        out_specs=P(("groups", "slab"), None, None, None),
        check_vma=False,
    )
```

profile of v0, /device:TPU:0, one launch (start us, length us, event | category | flops | bytes accessed | tf_op | source)
XLA Modules:
  0.0 237.9 jit_solution(4232999026324326829)
XLA Ops:
  0.0 3.4 %fusion.80 = (bf16[4,32,16,384]{3,2,1,0:T(8,128)(2,1)}, bf16[4,32,16,384]{3,2,1,0:T(8,128)(2,1)S(1)}) fusion(bf16[8,32,16,384]{3,2,1,0:T(8,128)(2,1)} %param.11), kind=kLoop, calls=%fused_computation.120 | loop fusion | bytes 6291456 | tf_op jit(solution)/shard_map/slice | solution.py:130
  3.4 5.4 %collective-permute-start = (bf16[4,32,16,384]{3,2,1,0:T(8,128)(2,1)}, bf16[4,32,16,384]{3,2,1,0:T(8,128)(2,1)}, u32[]{:S(2)}, u32[]{:S(2)}) collective-permute-start(bf16[4,32,16,384]{3,2,1,0:T(8,128)(2,1)} %get-tuple-element.80), channel_id=1, source_target_pairs={{0,15},{1,0},{2,1},{3,2},{4,3},{5,4},{6,5},{7,6},{8,7},{9,8},{10,9... | collective-permute-start | bytes 4718600 | tf_op jit(solution)/shard_map/ppermute | solution.py:15
  9.8 17.3 %collective-permute-done = bf16[4,32,16,384]{3,2,1,0:T(8,128)(2,1)} collective-permute-done((bf16[4,32,16,384]{3,2,1,0:T(8,128)(2,1)}, bf16[4,32,16,384]{3,2,1,0:T(8,128)(2,1)}, u32[]{:S(2)}, u32[]{:S(2)}) %collective-permute-start) | collective-permute-done | bytes 1572896 | tf_op jit(solution)/shard_map/ppermute | solution.py:15
  27.1 1.7 fusion.53
  28.8 1.2 fusion.52
  30.0 1.6 slice.99
  31.6 3.7 %fusion.51 = bf16[8,32,16,384]{3,2,1,0:T(8,128)(2,1)S(1)} fusion(bf16[8,28,16,384]{3,2,1,0:T(8,128)(2,1)S(1)} %fusion.53, bf16[4,32,16,384]{3,2,1,0:T(8,128)(2,1)} %collective-permute-done, bf16[4,32,16,384]{3,2,1,0:T(8,128)(2,1)S(1)} %get-tuple-element.81, bf16[8,32,12,384]{3,2,1,0:T(8,128)(2,1)S(1)} %slice.99), kind=kLoop, calls=%fused_computation.62 | loop fusion | flops 12582912 | bytes 11403264 | tf_op jit(solution)/shard_map/jit(_roll_static)/concatenate | solution.py:132
  35.4 1.6 copy-done.1
  37.0 1.2 bitcast_reduce_fusion.1
  39.2 3.1 %fusion.47 = f32[4,2,8,8,8]{4,3,2,1,0:T(8,128)S(1)} fusion(f32[4,2,8,8,8]{4,3,2,1,0:T(8,128)S(1)} %broadcast_multiply_fusion, bf16[1,8,4,8,2,8,384]{6,5,4,3,2,1,0:T(8,128)(2,1)} %bitcast.147), kind=kLoop, calls=%fused_computation.56 | loop fusion | flops 6287360 | bytes 3178496 | tf_op jit(solution)/shard_map/reduce_sum | solution.py:22
  42.4 5.5 %copy.19 = f32[1,8,4,8,2,8,384]{6,5,3,1,4,2,0:T(8,128)} copy(bf16[1,8,4,8,2,8,384]{6,5,4,3,2,1,0:T(8,128)(2,1)} %bitcast.148) | data formatting | bytes 9437184 | tf_op jit(solution)/shard_map/convert_element_type | solution.py:242
  48.0 19.0 %all_gather.3 = bf16[128,768]{1,0:T(8,128)(2,1)S(1)} all-gather(bf16[8,768]{1,0:T(8,128)(2,1)S(1)} %convolution_convert_fusion.2), channel_id=1, replica_groups=mesh['groups'=2,'slab'=16] {'slab'}, dimensions={0}, use_global_device_ids=true | all-gather | bytes 208896 | tf_op jit(solution)/shard_map/all_gather | solution.py:165
  70.4 3.5 %fusion.39 = bf16[4096,384]{1,0:T(8,128)(2,1)S(1)} fusion(f32[1,8,4,8,2,8,384]{6,5,3,1,4,2,0:T(8,128)} %copy.19, f32[384]{0:T(512)S(1)} %copy-done.5, f32[4096]{0:T(1024)S(1)} %rsqrt.42, f32[4096]{0:T(1024)S(1)} %div.56), kind=kLoop, calls=%fused_computation.41 | loop fusion | flops 6291456 | bytes 9471488 | tf_op jit(solution)/shard_map/convert_element_type | solution.py:145
  73.9 7.8 %convolution_convert_fusion = bf16[4096,1152]{1,0:T(8,128)(2,1)} fusion(bf16[4096,384]{1,0:T(8,128)(2,1)S(1)} %fusion.39, bf16[384,1152]{1,0:T(8,128)(2,1)S(1)} %copy-done.8), kind=kOutput, calls=%fused_computation.35 | convolution fusion | flops 3628597248 | bytes 13467648 | tf_op jit(solution)/shard_map/dot_general | solution.py:146
  81.7 96.5 %while.10 = (s32[]{:T(128)}, bf16[8,512,384]{1,2,0:T(8,128)(2,1)}, bf16[8,512,1152]{2,1,0:T(8,128)(2,1)}, s32[8,512]{1,0:T(8,128)}, bf16[8,12,32]{2,1,0:T(8,128)(2,1)}, /*index=5*/bf16[8,12,32]{2,1,0:T(8,128)(2,1)}, s32[]{:T(128)}) while((s32[]{:T(128)}, bf16[8,512,384]{1,2,0:T(8,128)(2,1)}, bf16[8,512,1152]{2,1,0:T(8,128)(2,1)}, ...), condition=%wide.region_13.14_spmd, body=%wide.region_9.13_spmd.sunk | while | flops 439110400 | bytes 48986200 | solution.py:231
  81.7 1.4 constant_dynamic-slice_fusion.4
  84.8 2.1 select_reduce_fusion.2
  86.9 2.6 %fusion.112 = f32[12,512]{1,0:T(8,128)S(1)} fusion(f32[12,512,512]{1,2,0:T(8,128)S(1)} %get-tuple-element.143, f32[12,512]{1,0:T(8,128)S(1)} %get-tuple-element.144, pred[512,512]{0,1:T(8,128)(4,1)S(1)} %broadcast_compare_fusion.2), kind=kLoop, calls=%fused_computation.2.clone.1 | loop fusion | flops 12576768 | bytes 12894208 | tf_op jit(solution)/shard_map/while/body/eval_jaxpr/reduce_sum | solution.py:71
  90.4 2.6 %fusion.114 = bf16[512,12,32]{0,2,1:T(8,128)(2,1)S(1)} fusion(bf16[512,12,32]{0,2,1:T(8,128)(2,1)S(1)} %bitcast.152, f32[12,512,512]{1,2,0:T(8,128)S(1)} %get-tuple-element.143, f32[12,512]{1,0:T(8,128)S(1)} %get-tuple-element.144, pred[512,512]{0,1:T(8,128)(4,1)S(1)} %broadcast_compare_fusion.2, f32[512,12]{0,1:T(8,128)S(1)} %get-tuple-element.146, ...), kind=kOutput, calls=%fused_computation.10.clone.1 | convolution fusion | flops 214892544 | bytes 13731328 | tf_op jit(solution)/shard_map/while/body/eval_jaxpr/tlq,qto->lto/dot_general | solution.py:72
  93.0 0.8 constant_dynamic-update-slice_fusion.2
  93.8 1.4 constant_dynamic-slice_fusion.4
  96.8 2.1 select_reduce_fusion.2
  98.9 2.6 %fusion.112 = f32[12,512]{1,0:T(8,128)S(1)} fusion(f32[12,512,512]{1,2,0:T(8,128)S(1)} %get-tuple-element.143, f32[12,512]{1,0:T(8,128)S(1)} %get-tuple-element.144, pred[512,512]{0,1:T(8,128)(4,1)S(1)} %broadcast_compare_fusion.2), kind=kLoop, calls=%fused_computation.2.clone.1 | loop fusion | flops 12576768 | bytes 12894208 | tf_op jit(solution)/shard_map/while/body/eval_jaxpr/reduce_sum | solution.py:71
  102.4 2.6 %fusion.114 = bf16[512,12,32]{0,2,1:T(8,128)(2,1)S(1)} fusion(bf16[512,12,32]{0,2,1:T(8,128)(2,1)S(1)} %bitcast.152, f32[12,512,512]{1,2,0:T(8,128)S(1)} %get-tuple-element.143, f32[12,512]{1,0:T(8,128)S(1)} %get-tuple-element.144, pred[512,512]{0,1:T(8,128)(4,1)S(1)} %broadcast_compare_fusion.2, f32[512,12]{0,1:T(8,128)S(1)} %get-tuple-element.146, ...), kind=kOutput, calls=%fused_computation.10.clone.1 | convolution fusion | flops 214892544 | bytes 13731328 | tf_op jit(solution)/shard_map/while/body/eval_jaxpr/tlq,qto->lto/dot_general | solution.py:72
  105.1 0.8 constant_dynamic-update-slice_fusion.2
  105.9 1.4 constant_dynamic-slice_fusion.4
  108.9 2.1 select_reduce_fusion.2
  111.0 2.6 %fusion.112 = f32[12,512]{1,0:T(8,128)S(1)} fusion(f32[12,512,512]{1,2,0:T(8,128)S(1)} %get-tuple-element.143, f32[12,512]{1,0:T(8,128)S(1)} %get-tuple-element.144, pred[512,512]{0,1:T(8,128)(4,1)S(1)} %broadcast_compare_fusion.2), kind=kLoop, calls=%fused_computation.2.clone.1 | loop fusion | flops 12576768 | bytes 12894208 | tf_op jit(solution)/shard_map/while/body/eval_jaxpr/reduce_sum | solution.py:71
  114.5 2.6 %fusion.114 = bf16[512,12,32]{0,2,1:T(8,128)(2,1)S(1)} fusion(bf16[512,12,32]{0,2,1:T(8,128)(2,1)S(1)} %bitcast.152, f32[12,512,512]{1,2,0:T(8,128)S(1)} %get-tuple-element.143, f32[12,512]{1,0:T(8,128)S(1)} %get-tuple-element.144, pred[512,512]{0,1:T(8,128)(4,1)S(1)} %broadcast_compare_fusion.2, f32[512,12]{0,1:T(8,128)S(1)} %get-tuple-element.146, ...), kind=kOutput, calls=%fused_computation.10.clone.1 | convolution fusion | flops 214892544 | bytes 13731328 | tf_op jit(solution)/shard_map/while/body/eval_jaxpr/tlq,qto->lto/dot_general | solution.py:72
  117.1 0.8 constant_dynamic-update-slice_fusion.2
  117.9 1.4 constant_dynamic-slice_fusion.4
  121.0 2.1 select_reduce_fusion.2
  123.1 2.6 %fusion.112 = f32[12,512]{1,0:T(8,128)S(1)} fusion(f32[12,512,512]{1,2,0:T(8,128)S(1)} %get-tuple-element.143, f32[12,512]{1,0:T(8,128)S(1)} %get-tuple-element.144, pred[512,512]{0,1:T(8,128)(4,1)S(1)} %broadcast_compare_fusion.2), kind=kLoop, calls=%fused_computation.2.clone.1 | loop fusion | flops 12576768 | bytes 12894208 | tf_op jit(solution)/shard_map/while/body/eval_jaxpr/reduce_sum | solution.py:71
  126.6 2.6 %fusion.114 = bf16[512,12,32]{0,2,1:T(8,128)(2,1)S(1)} fusion(bf16[512,12,32]{0,2,1:T(8,128)(2,1)S(1)} %bitcast.152, f32[12,512,512]{1,2,0:T(8,128)S(1)} %get-tuple-element.143, f32[12,512]{1,0:T(8,128)S(1)} %get-tuple-element.144, pred[512,512]{0,1:T(8,128)(4,1)S(1)} %broadcast_compare_fusion.2, f32[512,12]{0,1:T(8,128)S(1)} %get-tuple-element.146, ...), kind=kOutput, calls=%fused_computation.10.clone.1 | convolution fusion | flops 214892544 | bytes 13731328 | tf_op jit(solution)/shard_map/while/body/eval_jaxpr/tlq,qto->lto/dot_general | solution.py:72
  129.2 0.8 constant_dynamic-update-slice_fusion.2
  130.0 1.4 constant_dynamic-slice_fusion.4
  133.0 2.1 select_reduce_fusion.2
  135.1 2.6 %fusion.112 = f32[12,512]{1,0:T(8,128)S(1)} fusion(f32[12,512,512]{1,2,0:T(8,128)S(1)} %get-tuple-element.143, f32[12,512]{1,0:T(8,128)S(1)} %get-tuple-element.144, pred[512,512]{0,1:T(8,128)(4,1)S(1)} %broadcast_compare_fusion.2), kind=kLoop, calls=%fused_computation.2.clone.1 | loop fusion | flops 12576768 | bytes 12894208 | tf_op jit(solution)/shard_map/while/body/eval_jaxpr/reduce_sum | solution.py:71
  138.6 2.6 %fusion.114 = bf16[512,12,32]{0,2,1:T(8,128)(2,1)S(1)} fusion(bf16[512,12,32]{0,2,1:T(8,128)(2,1)S(1)} %bitcast.152, f32[12,512,512]{1,2,0:T(8,128)S(1)} %get-tuple-element.143, f32[12,512]{1,0:T(8,128)S(1)} %get-tuple-element.144, pred[512,512]{0,1:T(8,128)(4,1)S(1)} %broadcast_compare_fusion.2, f32[512,12]{0,1:T(8,128)S(1)} %get-tuple-element.146, ...), kind=kOutput, calls=%fused_computation.10.clone.1 | convolution fusion | flops 214892544 | bytes 13731328 | tf_op jit(solution)/shard_map/while/body/eval_jaxpr/tlq,qto->lto/dot_general | solution.py:72
  141.3 0.8 constant_dynamic-update-slice_fusion.2
  142.1 1.4 constant_dynamic-slice_fusion.4
  145.1 2.1 select_reduce_fusion.2
  147.2 2.6 %fusion.112 = f32[12,512]{1,0:T(8,128)S(1)} fusion(f32[12,512,512]{1,2,0:T(8,128)S(1)} %get-tuple-element.143, f32[12,512]{1,0:T(8,128)S(1)} %get-tuple-element.144, pred[512,512]{0,1:T(8,128)(4,1)S(1)} %broadcast_compare_fusion.2), kind=kLoop, calls=%fused_computation.2.clone.1 | loop fusion | flops 12576768 | bytes 12894208 | tf_op jit(solution)/shard_map/while/body/eval_jaxpr/reduce_sum | solution.py:71
  150.7 2.6 %fusion.114 = bf16[512,12,32]{0,2,1:T(8,128)(2,1)S(1)} fusion(bf16[512,12,32]{0,2,1:T(8,128)(2,1)S(1)} %bitcast.152, f32[12,512,512]{1,2,0:T(8,128)S(1)} %get-tuple-element.143, f32[12,512]{1,0:T(8,128)S(1)} %get-tuple-element.144, pred[512,512]{0,1:T(8,128)(4,1)S(1)} %broadcast_compare_fusion.2, f32[512,12]{0,1:T(8,128)S(1)} %get-tuple-element.146, ...), kind=kOutput, calls=%fused_computation.10.clone.1 | convolution fusion | flops 214892544 | bytes 13731328 | tf_op jit(solution)/shard_map/while/body/eval_jaxpr/tlq,qto->lto/dot_general | solution.py:72
  153.3 0.8 constant_dynamic-update-slice_fusion.2
  154.1 1.4 constant_dynamic-slice_fusion.4
  157.2 2.1 select_reduce_fusion.2
  159.3 2.6 %fusion.112 = f32[12,512]{1,0:T(8,128)S(1)} fusion(f32[12,512,512]{1,2,0:T(8,128)S(1)} %get-tuple-element.143, f32[12,512]{1,0:T(8,128)S(1)} %get-tuple-element.144, pred[512,512]{0,1:T(8,128)(4,1)S(1)} %broadcast_compare_fusion.2), kind=kLoop, calls=%fused_computation.2.clone.1 | loop fusion | flops 12576768 | bytes 12894208 | tf_op jit(solution)/shard_map/while/body/eval_jaxpr/reduce_sum | solution.py:71
  162.8 2.6 %fusion.114 = bf16[512,12,32]{0,2,1:T(8,128)(2,1)S(1)} fusion(bf16[512,12,32]{0,2,1:T(8,128)(2,1)S(1)} %bitcast.152, f32[12,512,512]{1,2,0:T(8,128)S(1)} %get-tuple-element.143, f32[12,512]{1,0:T(8,128)S(1)} %get-tuple-element.144, pred[512,512]{0,1:T(8,128)(4,1)S(1)} %broadcast_compare_fusion.2, f32[512,12]{0,1:T(8,128)S(1)} %get-tuple-element.146, ...), kind=kOutput, calls=%fused_computation.10.clone.1 | convolution fusion | flops 214892544 | bytes 13731328 | tf_op jit(solution)/shard_map/while/body/eval_jaxpr/tlq,qto->lto/dot_general | solution.py:72
  165.4 0.8 constant_dynamic-update-slice_fusion.2
  166.2 1.4 constant_dynamic-slice_fusion.4
  169.2 2.1 select_reduce_fusion.2
  171.3 2.6 %fusion.112 = f32[12,512]{1,0:T(8,128)S(1)} fusion(f32[12,512,512]{1,2,0:T(8,128)S(1)} %get-tuple-element.143, f32[12,512]{1,0:T(8,128)S(1)} %get-tuple-element.144, pred[512,512]{0,1:T(8,128)(4,1)S(1)} %broadcast_compare_fusion.2), kind=kLoop, calls=%fused_computation.2.clone.1 | loop fusion | flops 12576768 | bytes 12894208 | tf_op jit(solution)/shard_map/while/body/eval_jaxpr/reduce_sum | solution.py:71
  174.8 2.6 %fusion.114 = bf16[512,12,32]{0,2,1:T(8,128)(2,1)S(1)} fusion(bf16[512,12,32]{0,2,1:T(8,128)(2,1)S(1)} %bitcast.152, f32[12,512,512]{1,2,0:T(8,128)S(1)} %get-tuple-element.143, f32[12,512]{1,0:T(8,128)S(1)} %get-tuple-element.144, pred[512,512]{0,1:T(8,128)(4,1)S(1)} %broadcast_compare_fusion.2, f32[512,12]{0,1:T(8,128)S(1)} %get-tuple-element.146, ...), kind=kOutput, calls=%fused_computation.10.clone.1 | convolution fusion | flops 214892544 | bytes 13731328 | tf_op jit(solution)/shard_map/while/body/eval_jaxpr/tlq,qto->lto/dot_general | solution.py:72
  177.5 0.8 constant_dynamic-update-slice_fusion.2
  178.3 4.2 %fusion.59 = f32[8,512,384]{2,1,0:T(8,128)S(1)} fusion(bf16[8,512,384]{1,2,0:T(8,128)(2,1)} %get-tuple-element.37, bf16[384,384]{1,0:T(8,128)(2,1)} %param.17), kind=kOutput, calls=%fused_computation.80 | convolution fusion | flops 1207959552 | bytes 9732096 | tf_op jit(solution)/shard_map/dot_general | solution.py:235
  182.5 2.5 %convert_reduce_fusion = (f32[8,512]{1,0:T(8,128)S(1)}, bf16[8,512,384]{2,1,0:T(8,128)(2,1)}) fusion(f32[8,384]{1,0:T(8,128)S(1)} %get-tuple-element.92, f32[8,512,384]{2,1,0:T(8,128)S(1)} %bitcast.145, f32[8,512,384]{2,1,0:T(8,128)S(1)} %fusion.59), kind=kLoop, calls=%fused_computation.45 | loop fusion | flops 7860224 | bytes 15757312 | tf_op jit(solution)/shard_map/reduce_sum | solution.py:20
  185.0 3.0 %fusion.41 = f32[8,512]{1,0:T(8,128)S(1)} fusion(bf16[8,512,384]{2,1,0:T(8,128)(2,1)} %get-tuple-element.68, f32[8,512]{1,0:T(8,128)S(1)} %get-tuple-element.85), kind=kLoop, calls=%fused_computation.47 | loop fusion | flops 6287360 | bytes 3178496 | tf_op jit(solution)/shard_map/reduce_sum | solution.py:22
  188.1 2.4 %fusion.44 = bf16[4096,384]{1,0:T(8,128)(2,1)} fusion(bf16[8,512,384]{2,1,0:T(8,128)(2,1)S(1)} %copy-done.2, f32[384]{0:T(512)S(1)} %copy-done.4, f32[4096]{0:T(1024)S(1)} %bitcast.159, f32[4096]{0:T(1024)S(1)} %bitcast.160), kind=kLoop, calls=%fused_computation.50 | loop fusion | flops 7864320 | bytes 6325760 | tf_op jit(solution)/shard_map/convert_element_type | solution.py:245
  190.5 18.1 %fusion.45 = bf16[4096,384]{1,0:T(8,128)(2,1)} fusion(bf16[8,512,384]{2,1,0:T(8,128)(2,1)} %get-tuple-element.68, bf16[1536,384]{1,0:T(8,128)(2,1)S(1)} %copy-done, bf16[4096,384]{1,0:T(8,128)(2,1)} %fusion.44, bf16[384,1536]{1,0:T(8,128)(2,1)S(1)} %copy-done.6), kind=kOutput, calls=%fused_computation.51 | convolution fusion | flops 9725018112 | bytes 11796480 | tf_op jit(solution)/shard_map/dot_general | solution.py:250
  208.7 2.3 copy.26
  211.3 1.7 fusion.50
  213.5 22.4 %collective-permute-done.1 = bf16[4,32,16,384]{3,2,1,0:T(8,128)(2,1)S(1)} collective-permute-done((bf16[4,32,16,384]{3,2,1,0:T(8,128)(2,1)S(1)}, bf16[4,32,16,384]{3,2,1,0:T(8,128)(2,1)S(1)}, u32[]{:S(2)}, u32[]{:S(2)}) %collective-permute-start.1) | collective-permute-done | bytes 1572896 | tf_op jit(solution)/shard_map/ppermute | solution.py:15
  235.8 2.0 pad_maximum_fusion.5
  (125 shorter events, 26.9 us)
Async XLA Ops:
  0.0 190.5 %copy-start = (bf16[1536,384]{1,0:T(8,128)(2,1)S(1)}, bf16[1536,384]{1,0:T(8,128)(2,1)}, u32[]{:S(2)}) copy-start(bf16[1536,384]{1,0:T(8,128)(2,1)} %param.19) | copy-start | bytes 3538948
  3.4 23.7 %collective-permute-start = (bf16[4,32,16,384]{3,2,1,0:T(8,128)(2,1)}, bf16[4,32,16,384]{3,2,1,0:T(8,128)(2,1)}, u32[]{:S(2)}, u32[]{:S(2)}) collective-permute-start(bf16[4,32,16,384]{3,2,1,0:T(8,128)(2,1)} %get-tuple-element.80), channel_id=1, source_target_pairs={{0,15},{1,0},{2,1},{3,2},{4,3},{5,4},{6,5},{7,6},{8,7},{9,8},{10,9... | collective-permute-start | bytes 4718600 | tf_op jit(solution)/shard_map/ppermute | solution.py:15
  35.3 1.7 copy-start.1
  35.3 3.4 %copy-start.5 = (f32[384]{0:T(512)S(1)}, f32[384]{0:T(512)}, u32[]{:S(2)}) copy-start(f32[384]{0:T(512)} %param.12) | copy-start | bytes 4612
  35.4 3.3 %copy-start.7 = (bf16[384,1152]{1,0:T(8,128)(2,1)S(1)}, bf16[384,1152]{1,0:T(8,128)(2,1)}, u32[]{:S(2)}) copy-start(bf16[384,1152]{1,0:T(8,128)(2,1)} %param.14) | copy-start | bytes 2654212
  42.4 25.7 %copy-start.3 = (bf16[384,384]{1,0:T(8,128)(2,1)S(1)}, bf16[384,384]{1,0:T(8,128)(2,1)}, u32[]{:S(2)}) copy-start(bf16[384,384]{1,0:T(8,128)(2,1)} %param.15) | copy-start | bytes 884740
  42.4 26.2 %copy-start.8 = (bf16[384,1152]{1,0:T(8,128)(2,1)S(1)}, bf16[384,1152]{1,0:T(8,128)(2,1)}, u32[]{:S(2)}) copy-start(bf16[384,1152]{1,0:T(8,128)(2,1)} %param.16) | copy-start | bytes 2654212
  178.3 4.2 %slice-start = ((s8[6291456]{0:T(1024)(128)(4,1)}), s8[4194304]{0:T(1024)(128)(4,1)S(1)}, s32[]{:S(2)}) async-start(s8[6291456]{0:T(1024)(128)(4,1)} %bitcast.143), calls=%async_computation | async-start | bytes 8388608
  178.3 4.2 %slice-start.1 = ((s8[6291456]{0:T(1024)(128)(4,1)}), s8[2097152]{0:T(1024)(128)(4,1)S(1)}, s32[]{:S(2)}) async-start(s8[6291456]{0:T(1024)(128)(4,1)} %bitcast.143), calls=%async_computation.1 | async-start | bytes 4194304
  185.0 3.1 %copy-start.2 = (bf16[8,512,384]{2,1,0:T(8,128)(2,1)S(1)}, bf16[8,512,384]{2,1,0:T(8,128)(2,1)}, u32[]{:S(2)}) copy-start(bf16[8,512,384]{2,1,0:T(8,128)(2,1)} %get-tuple-element.68) | copy-start | bytes 9437188
  185.0 3.1 %copy-start.4 = (f32[384]{0:T(512)S(1)}, f32[384]{0:T(512)}, u32[]{:S(2)}) copy-start(f32[384]{0:T(512)} %param.13) | copy-start | bytes 4612
  188.1 2.4 %copy-start.6 = (bf16[384,1536]{1,0:T(8,128)(2,1)S(1)}, bf16[384,1536]{1,0:T(8,128)(2,1)}, u32[]{:S(2)}) copy-start(bf16[384,1536]{1,0:T(8,128)(2,1)} %param.18) | copy-start | bytes 3538948
  213.3 22.6 %collective-permute-start.1 = (bf16[4,32,16,384]{3,2,1,0:T(8,128)(2,1)S(1)}, bf16[4,32,16,384]{3,2,1,0:T(8,128)(2,1)S(1)}, u32[]{:S(2)}, u32[]{:S(2)}) collective-permute-start(bf16[4,32,16,384]{3,2,1,0:T(8,128)(2,1)S(1)} %get-tuple-element.78), channel_id=1, source_target_pairs={{0,1},{1,2},{2,3},{3,4},{4,5},{5,6},{6,7},{7,8},{8,9},{9,10},{10,1... | collective-permute-start | bytes 4718600 | tf_op jit(solution)/shard_map/ppermute | solution.py:15
where the time goes:
time: 239 us; the launch traced here: 238 us
  matrix products  69.3 us (29%)
  other arithmetic  56.7 us (24%)
  local copies, waits for them, and re-layouts  46.8 us (20%)
  waiting for transfers between devices  39.7 us (17%)
  blocking collectives  19 us (8%)
  starting transfers between devices  5.65 us (2%)
    ppermute x2, waiting for transfers between devices, shifted_2(): return lax.ppermute(value, axis, pairs)  39.7 us
    dynamic_slice x24, local copies, waits for them, and re-layouts, body(): lax.map(lone_region, (stacked_entries, region_identifiers, courier_lookup...  21.7 us
    dot_general x8, matrix products, window_local(): jnp.einsum('tlq,qto->lto', weights.astype(jnp.bfloat16), value_rows, pref...  20.9 us
    reduce_sum x8, other arithmetic, window_local(): ongoing_totals = jnp.sum(weights, axis=-1)  20.6 us
    all_gather x1, blocking collectives, body(): piece = lax.all_gather(kv_local, 'slab', axis=0, tiled=True)  19 us
    dot_general x1, matrix products, body(): jnp.dot(hidden, perceptron_exit_projection, preferred_element_type=jnp.fl...  18.1 us
    dot_general x8, matrix products, window_local(): jnp.einsum('cfm,rfm->fcr', asking_table, source_table, preferred_element_...  16.8 us
    dot_general x1, matrix products, body(): jnp.dot(tok_normed.reshape(-1, EMBED_BREADTH), region_triple_projection,...  7.79 us
  transfers between devices with their start and end apart: 2, of which 2 were waited for; matrix products, arithmetic and copies ran while one was open for 0% of the time, Pallas kernels for 0%

commit v1 on v0

v1 whole, which is shorter than its diff:
```python
import functools

import jax
import jax.numpy as jnp
from jax import lax
from jax.experimental import pallas as pl
from jax.experimental.pallas import tpu as pltpu
from jax.sharding import PartitionSpec as P

C = 384
HEADS = 12
HD = 32
WIN = 8
HALF = 4
GROUPS = C // 128
BIG = 2.0**100
LOG2E = 1.4426950408889634


def shifted(value, axis, steps):
    count = lax.axis_size(axis)
    pairs = [(source, (source + steps) % count) for source in range(count)]
    return lax.ppermute(value, axis, pairs)


def norm(values, gain):
    values = values.astype(jnp.float32)
    centre = jnp.mean(values, axis=-1, keepdims=True)
    moved = values - centre
    spread = jnp.mean(moved * moved, axis=-1, keepdims=True)
    return moved * lax.rsqrt(spread + 1e-05) * gain


def dot_t(a, b):
    return lax.dot_general(a, b, (((1,), (1,)), ((), ())), preferred_element_type=jnp.float32)


def strip_kernel(
    first,
    strips,
    last_ref,
    loc_a,
    loc_b,
    halo_a,
    halo_b,
    g1,
    g2,
    wqkv,
    wo,
    w1,
    w2,
    delta,
    kc,
    vc,
    out_loc,
    out_halo,
    x_s,
    qkv_s,
    att_s,
    y_s,
):
    strip = pl.program_id(0) + first
    rows = 2 * WIN**3
    half = WIN**3
    tokens = jnp.concatenate(
        [r[...].reshape(rows // 4, C).astype(jnp.float32) for r in (loc_a, loc_b, halo_a, halo_b)],
        axis=0,
    )
    tokens = pltpu.roll(tokens, rows - HALF, 0).reshape(rows // 16, 2, 8, C)
    gain1 = g1[...]
    for w in range(2):
        x_w = tokens[:, w].reshape(half, C)
        x_s[w] = x_w
        n_w = norm(x_w, gain1).astype(jnp.bfloat16)
        for part in range(3):
            proj = jnp.dot(
                n_w, wqkv[:, part * C : (part + 1) * C], preferred_element_type=jnp.float32
            )
            if part == 0:
                proj = proj * (HD**-0.5 * LOG2E)
            proj = proj.astype(jnp.bfloat16)
            for g in range(GROUPS):
                qkv_s[part, w, g] = proj[:, g * 128 : (g + 1) * 128]

    lane = lax.broadcasted_iota(jnp.int32, (1, 128), 1)
    zflag = last_ref[0]
    yflag = jnp.where(strip == strips - 1, 1, 0)

    def attend(step, carry):
        w = step // GROUPS
        g = step % GROUPS
        row = lax.broadcasted_iota(jnp.int32, (half, 128), 0)
        col = lax.broadcasted_iota(jnp.int32, (half, 128), 1)
        t = ((row // 8) * 16 + row % 8 + w * 8 + HALF) & (rows - 1)
        label = (
            (t // half) * 4 * zflag
            + ((t // (half // 2)) & 1) * 2 * yflag
            + jnp.where((t & 15) < HALF, w, 0)
        )
        same = label == col
        feat_q = jnp.where(same, 0.0, -BIG).astype(jnp.bfloat16)
        feat_k = jnp.where(same, 1.0, 0.0).astype(jnp.bfloat16)
        q4 = qkv_s[0, w, g]
        k4 = qkv_s[1, w, g]
        v4 = qkv_s[2, w, g]
        k_aug = jnp.concatenate([k4, feat_k], axis=1)
        acc = jnp.zeros((half, 256), jnp.float32)
        peak = jnp.zeros((half, 128), jnp.float32)
        zero = jnp.zeros((), jnp.bfloat16)
        for h in range(4):
            mine = (lane // HD) == h
            mask = jnp.where(mine, 1.0, 0.0).astype(jnp.bfloat16)
            q_aug = jnp.concatenate([q4 * mask, feat_q], axis=1)
            s = dot_t(q_aug, k_aug)
            m = jnp.max(s, axis=1, keepdims=True)
            p = jnp.exp2(s - m).astype(jnp.bfloat16)
            v_aug = jnp.concatenate([v4 * mask, jnp.broadcast_to(mask, (half, 128))], axis=1)
            acc = acc + jnp.dot(p, v_aug, preferred_element_type=jnp.float32)
            peak = jnp.where(mine, m, peak)
        kcw = kc[0, pl.ds(w, 1), g]
        vcw = vc[0, pl.ds(w, 1), g]
        r128 = lax.broadcasted_iota(jnp.int32, (128, 128), 0)
        c128 = lax.broadcasted_iota(jnp.int32, (128, 128), 1)
        k_mat = jnp.where(r128 // HD == c128 // HD, kcw, 0.0).astype(jnp.bfloat16)
        c4 = dot_t(q4, k_mat)
        top = jnp.maximum(peak, c4)
        a = jnp.exp2(peak - top)
        e = jnp.exp2(c4 - top)
        att = (acc[:, :128] * a + e * vcw) / (acc[:, 128:] * a + e)
        att_s[w, g] = att.astype(jnp.bfloat16)
        return carry

    lax.fori_loop(0, 2 * GROUPS, attend, 0)

    gain2 = g2[...]
    tile = half // 2

    def finish(step, carry):
        w = step // 2
        part = step % 2
        at = pl.ds(pl.multiple_of(part * tile, tile), tile)
        att = jnp.concatenate([att_s[w, g, at] for g in range(GROUPS)], axis=1)
        mixed = x_s[w, at] + jnp.dot(att, wo[...], preferred_element_type=jnp.float32)
        mixed = (mixed + delta[0, pl.ds(w, 1)]).astype(jnp.bfloat16).astype(jnp.float32)
        n = norm(mixed, gain2).astype(jnp.bfloat16)
        u = jnp.dot(n, w1[...], preferred_element_type=jnp.float32)
        hidden = 0.5 * u * (1.0 + jnp.tanh((2.0 / jnp.pi) ** 0.5 * (u + 0.044715 * (u * u * u))))
        out = mixed + jnp.dot(
            hidden.astype(jnp.bfloat16), w2[...], preferred_element_type=jnp.float32
        )
        y_s[pl.ds(part * (tile // 8), tile // 8), w] = out.reshape(tile // 8, 8, C)
        return carry

    lax.fori_loop(0, 4, finish, 0)
    done = pltpu.roll(y_s[...].reshape(rows, C), HALF, 0).astype(jnp.bfloat16)
    done = done.reshape(4, HALF, HALF * 16, C)
    ya = 2 * pl.program_id(0)
    out_loc[:, ya] = done[0]
    out_loc[:, ya + 1] = done[1]
    out_halo[:, ya] = done[2]
    out_halo[:, ya + 1] = done[3]


def strips_call(first, count, strips, last, volume, halo, halo_first, g1, g2, ws, delta, kc, vc):
    yh = 2 * strips

    def block(plane, offset):
        return pl.BlockSpec(
            (HALF, 1, HALF * 16, C), lambda b: (plane, (2 * (b + first) + offset) % yh, 0, 0)
        )

    def halo_block(offset):
        return pl.BlockSpec((HALF, 1, HALF * 16, C), lambda b: (0, 2 * b + offset + halo_first, 0, 0))

    def whole(a):
        return pl.BlockSpec(a.shape, lambda b: (0,) * a.ndim)

    per = [
        pl.BlockSpec((1,) + a.shape[1:], lambda b, n=a.ndim: (b + first,) + (0,) * (n - 1))
        for a in (delta, kc, vc)
    ]
    half = WIN**3
    shape = jax.ShapeDtypeStruct((HALF, 2 * count, HALF * 16, C), jnp.bfloat16)
    out_spec = pl.BlockSpec(shape.shape, lambda b: (0, 0, 0, 0))
    flops = count * 2 * half * 2 * (C * 3 * C + C * C + 2 * C * 4 * C + HEADS * half * 320)
    return pl.pallas_call(
        functools.partial(strip_kernel, first, strips),
        grid=(count,),
        out_shape=(shape, shape),
        in_specs=[
            pl.BlockSpec(memory_space=pltpu.SMEM),
            block(1, 1),
            block(1, 2),
            halo_block(0),
            halo_block(1),
            whole(g1),
            whole(g2),
        ]
        + [whole(w) for w in ws]
        + per,
        out_specs=(out_spec, out_spec),
        scratch_shapes=[
            pltpu.VMEM((2, half, C), jnp.float32),
            pltpu.VMEM((3, 2, GROUPS, half, 128), jnp.bfloat16),
            pltpu.VMEM((2, GROUPS, half, 128), jnp.bfloat16),
            pltpu.VMEM((2 * half // 16, 2, 8, C), jnp.float32),
        ],
        compiler_params=pltpu.CompilerParams(
            dimension_semantics=("arbitrary",), vmem_limit_bytes=48 * 1024 * 1024
        ),
        cost_estimate=pl.CostEstimate(
            flops=flops,
            bytes_accessed=count * 4 * 2 * half * C * 2,
            transcendentals=count * 2 * half * (HEADS * half + 4 * C),
        ),
        name="strips",
    )(last, volume, volume, halo, halo, g1, g2, *ws, delta, kc, vc)


def carriers(volume, g1, wc, wco, wr):
    planes, yh = volume.shape[:2]
    strips = yh // 2
    parts = volume.astype(jnp.float32).reshape(2, HALF, yh, HALF, 16, C).sum(axis=(1, 3))
    inner = parts[:, :, 4:12].sum(axis=2)
    outer = parts[:, :, :4].sum(axis=2) + parts[:, :, 12:].sum(axis=2)
    sums = jnp.stack([inner, outer], axis=2)
    sums = jnp.roll(sums, -1, axis=1).reshape(2, strips, 2, 2, C).sum(axis=2)
    sums = sums.reshape(2, strips * 2, C)
    arrived = shifted(sums[0], "slab", -1)
    carrier = (sums[1] + arrived) * (1.0 / WIN**3)
    count = carrier.shape[0]
    normed = norm(carrier, g1).astype(jnp.bfloat16)
    proj = jnp.dot(normed, wc, preferred_element_type=jnp.float32).astype(jnp.bfloat16)
    asking = proj[:, :C].reshape(count, HEADS, HD)
    everyone = lax.all_gather(proj[:, C:], "slab", axis=0, tiled=True)
    keys = everyone[:, :C].reshape(-1, HEADS, HD)
    values = everyone[:, C:].reshape(-1, HEADS, HD).astype(jnp.float32)
    s = jnp.einsum("chd,rhd->hcr", asking, keys, preferred_element_type=jnp.float32) * HD**-0.5
    weights = jax.nn.softmax(s, axis=-1)
    mix = jnp.einsum("hcr,rhd->chd", weights, values, precision=lax.Precision.HIGHEST)
    mix = mix.reshape(count, C).astype(jnp.bfloat16)
    delta = jnp.dot(mix, wco, preferred_element_type=jnp.float32)
    kv = jnp.dot(
        norm(carrier + delta, g1).astype(jnp.bfloat16), wr[:, C:], preferred_element_type=jnp.float32
    ).astype(jnp.bfloat16)
    kv = kv.astype(jnp.float32)
    kc = kv[:, :C].reshape(strips, 2, GROUPS, 128)
    vc = kv[:, C:].reshape(strips, 2, GROUPS, 128)
    return delta.reshape(strips, 2, C), kc, vc


CALLS = 1


def body(volume_features, g1, g2, wc, wco, wr, wro, w1, w2):
    planes, ny, nx, channels = volume_features.shape
    yh = ny // HALF
    strips = yh // 2
    volume = volume_features.reshape(planes, yh, HALF * nx, channels)
    position = lax.axis_index("slab")
    last = (position == lax.axis_size("slab") - 1).astype(jnp.int32).reshape(1)
    sent = jnp.concatenate([volume[:HALF, 1:], volume[:HALF, :1]], axis=1)
    per = strips // CALLS
    halos = [shifted(sent[:, 2 * per * i : 2 * per * (i + 1)], "slab", -1) for i in range(CALLS)]
    delta, kc, vc = carriers(volume, g1, wc, wco, wr)
    gains = (g1.reshape(1, channels), g2.reshape(1, channels))
    ws = (wr, wro, w1, w2)
    local, returned = [], []
    for i in range(CALLS):
        out_loc, out_halo = strips_call(
            i * per, per, strips, last, volume, halos[i], 0, *gains, ws, delta, kc, vc
        )
        local.append(out_loc)
        returned.append(shifted(out_halo, "slab", 1))
    local = jnp.concatenate(local, axis=1)
    returned = jnp.concatenate(returned, axis=1)
    done = jnp.concatenate([returned, local], axis=0)
    done = jnp.concatenate([done[:, -1:], done[:, :-1]], axis=1)
    return done.reshape(volume_features.shape)


def solution(mesh):
    placed = (P(("groups", "slab"), None, None, None),) + (P(),) * 8
    return jax.shard_map(
        body,
        mesh=mesh,
        in_specs=placed,
        out_specs=P(("groups", "slab"), None, None, None),
        check_vma=False,
    )
```

time: 239 us -> 167 us (0.70)
  Pallas kernels: 0 us -> 88.4 us
  matrix products: 69.3 us -> 3.03 us
  other arithmetic: 56.7 us -> 6.84 us
  local copies, waits for them, and re-layouts: 46.8 us -> 6.2 us
  waiting for transfers between devices: 39.7 us -> 22.4 us
  blocking collectives: 19 us -> 32.8 us
    pallas_call x0 -> x1, Pallas kernels: none -> 88.4 us  [strips_call(): pl.pallas_call(functools.partial(strip_kernel, first, strips), grid=(coun...]
    dot_general x25 -> x5, matrix products: 69.3 us -> 3.03 us  [the longest x1 1.23 us: carriers(): delta = jnp.dot(mix, wco, preferred_element_type=jnp.float32)]
    reduce_sum x24 -> x8, other arithmetic: 32.6 us -> 3.45 us  [the longest x1 2.53 us: carriers(): volume.astype(jnp.float32).reshape(2, HALF, yh, HALF, 16, C)]
    dynamic_slice x24 -> x0, local copies, waits for them, and re-layouts: 21.7 us -> none  [body(): lax.map(lone_region, (stacked_entries, region_identifiers, courier_lookup...]
    ppermute x2 -> x3, waiting for transfers between devices: 39.7 us -> 22.4 us  [shifted(): return lax.ppermute(value, axis, pairs)]
    all_gather x1, blocking collectives: 19 us -> 32.8 us  [carriers(): everyone = lax.all_gather(proj[:, C:], 'slab', axis=0, tiled=True)]
    concatenate x5 -> x3, other arithmetic: 10.3 us -> 3.35 us  [the longest x1 2.02 us: body(): done = jnp.concatenate([done[:, -1:], done[:, :-1]], axis=1)]
    dynamic_update_slice x8 -> x0, local copies, waits for them, and re-layouts: 6.32 us -> none  [body(): lax.map(lone_region, (stacked_entries, region_identifiers, courier_lookup...]
  transfers between devices with their start and end apart: 2 -> 3, of which waited for: 2 -> 1; matrix products, arithmetic and copies ran while one was open for 0% -> 5% of each run, Pallas kernels for 0% -> 0%
where the time goes in v1:
time: 167 us; the launch traced here: 166 us
  Pallas kernels  88.4 us (53%)
  blocking collectives  32.8 us (20%)
  waiting for transfers between devices  22.4 us (13%)
  other arithmetic  6.84 us (4%)
  starting transfers between devices  6.51 us (4%)
  local copies, waits for them, and re-layouts  6.2 us (4%)
  matrix products  3.03 us (2%)
    pallas_call x1, Pallas kernels, strips_call(): pl.pallas_call(functools.partial(strip_kernel, first, strips), grid=(coun...  88.4 us
    all_gather x1, blocking collectives, carriers(): everyone = lax.all_gather(proj[:, C:], 'slab', axis=0, tiled=True)  32.8 us
    ppermute x3, waiting for transfers between devices, shifted(): return lax.ppermute(value, axis, pairs)  22.4 us
    ppermute x3, starting transfers between devices, shifted(): return lax.ppermute(value, axis, pairs)  6.51 us
  transfers between devices with their start and end apart: 3, of which 1 were waited for; matrix products, arithmetic and copies ran while one was open for 5% of the time, Pallas kernels for 0%

profile of v1, /device:TPU:0, one launch (start us, length us, event | category | flops | bytes accessed | tf_op | source)
XLA Modules:
  0.0 166.5 jit_solution(4912601247377351462)
XLA Ops:
  0.0 0.0 copy-start
  0.0 2.5 %convert_reduce_fusion = f32[2,8,16,384]{3,2,1,0:T(8,128)S(1)} fusion(bf16[2,4,8,4,16,384]{5,4,3,2,1,0:T(8,128)(2,1)} %bitcast.25), kind=kLoop, calls=%fused_computation | loop fusion | flops 3047424 | bytes 3538944 | tf_op jit(solution)/shard_map/reduce_sum | solution.py:223
  2.5 0.1 slice_reduce_fusion
  2.6 0.1 slice_reduce_fusion.1
  2.8 0.1 reduce_sum.94
  2.9 5.5 %collective-permute-start.1 = (f32[8,384]{1,0:T(8,128)S(1)}, f32[8,384]{1,0:T(8,128)S(1)}, u32[]{:S(2)}, u32[]{:S(2)}) collective-permute-start(f32[8,384]{1,0:T(8,128)S(1)} %squeeze.7), channel_id=1, source_target_pairs={{0,15},{1,0},{2,1},{3,2},{4,3},{5,4},{6,5},{7,6},{8,7},{9,8},{10,9... | collective-permute-start | bytes 36872 | tf_op jit(solution)/shard_map/ppermute | solution.py:23
  8.4 0.9 slice.77
  9.4 0.0 copy-start.7
  9.4 0.0 copy-start.6
  9.4 1.5 slice.76
  10.9 0.0 copy-start.1
  10.9 1.3 pad_maximum_fusion.1
  12.2 0.0 copy-start.2
  12.2 0.0 copy-start.4
  12.2 0.7 collective-permute-start
  12.9 0.0 copy-done.7
  12.9 0.0 copy-done.6
  13.0 0.0 collective-permute-done.1
  13.0 0.1 fusion.16
  13.1 0.0 copy-start.5
  13.1 0.2 multiply_reduce_fusion.1
  13.3 0.4 copy-done.5
  13.7 0.0 copy-done
  13.7 0.3 convolution_convert_fusion
  14.0 0.7 reshape.95
  14.7 32.8 %all_gather.3 = bf16[128,768]{1,0:T(8,128)(2,1)S(1)} all-gather(bf16[8,768]{1,0:T(8,128)(2,1)S(1)} %slice.85), channel_id=1, replica_groups=mesh['groups'=2,'slab'=16] {'slab'}, dimensions={0}, use_global_device_ids=true | all-gather | bytes 208896 | tf_op jit(solution)/shard_map/all_gather | solution.py:235
  47.5 0.1 copy.31
  47.6 0.1 copy.30
  47.8 1.0 fusion.19
  48.7 0.2 fusion.5
  48.9 0.3 fusion
  49.3 0.1 convert_element_type.39
  49.4 1.2 fusion.15
  50.6 0.2 multiply_reduce_fusion
  50.8 0.0 copy-done.1
  50.8 0.2 fusion.1
  51.1 0.0 collective-permute-done.halo_a.halo_b
  51.1 0.0 copy-done.2
  51.1 0.0 copy-done.4
  51.1 0.0 copy-start.3
  51.2 1.3 copy-done.3
  52.4 88.4 %strips.1 = (bf16[4,8,64,384]{3,2,1,0:T(8,128)(2,1)S(1)}, bf16[4,8,64,384]{3,2,1,0:T(8,128)(2,1)}) custom-call(s32[1]{0:T(128)} %bitcast.last_ref, bf16[8,8,64,384]{3,2,1,0:T(8,128)(2,1)} %bitcast.28, bf16[8,8,64,384]{3,2,1,0:T(8,128)(2,1)} %bitcast.29, bf16[4,8,64,384]{3,2,1,0:T(8,128)(2,1)} %collective-permute-done.halo_a.halo_b, ...), custom_call_target="tpu_custom_call" | custom-call | flops 30601641984 | bytes 12582912 | tf_op jit(solution)/shard_map/strips/pallas_call | solution.py:186
  140.8 0.3 collective-permute-start.2
  141.1 22.4 %collective-permute-done.2 = bf16[4,8,64,384]{3,2,1,0:T(8,128)(2,1)S(1)} collective-permute-done((bf16[4,8,64,384]{3,2,1,0:T(8,128)(2,1)}, bf16[4,8,64,384]{3,2,1,0:T(8,128)(2,1)S(1)}, u32[]{:S(2)}, u32[]{:S(2)}) %collective-permute-start.2) | collective-permute-done | bytes 1572896 | tf_op jit(solution)/shard_map/ppermute | solution.py:23
  163.5 0.2 constant_dynamic-update-slice_fusion.1
  163.7 0.3 constant_dynamic-update-slice_fusion
  164.1 0.3 slice.92
  164.4 2.0 %pad_maximum_fusion = bf16[8,8,64,384]{3,2,1,0:T(8,128)(2,1)} fusion(bf16[8,7,64,384]{3,2,1,0:T(8,128)(2,1)S(1)} %slice.92, bf16[8,1,64,384]{3,2,1,0:T(8,128)(2,1)S(1)} %slice.91), kind=kLoop, calls=%fused_computation.1 | loop fusion | flops 1572864 | bytes 6291456 | tf_op jit(solution)/shard_map/concatenate | solution.py:278
  (24 shorter events, 0.3 us)
Async XLA Ops:
  0.0 13.7 %copy-start = (bf16[384,1152]{1,0:T(8,128)(2,1)S(1)}, bf16[384,1152]{1,0:T(8,128)(2,1)}, u32[]{:S(2)}) copy-start(bf16[384,1152]{1,0:T(8,128)(2,1)} %param.12) | copy-start | bytes 2654212
  2.9 10.0 %collective-permute-start.1 = (f32[8,384]{1,0:T(8,128)S(1)}, f32[8,384]{1,0:T(8,128)S(1)}, u32[]{:S(2)}, u32[]{:S(2)}) collective-permute-start(f32[8,384]{1,0:T(8,128)S(1)} %squeeze.7), channel_id=1, source_target_pairs={{0,15},{1,0},{2,1},{3,2},{4,3},{5,4},{6,5},{7,6},{8,7},{9,8},{10,9... | collective-permute-start | bytes 36872 | tf_op jit(solution)/shard_map/ppermute | solution.py:23
  9.4 3.5 %copy-start.7 = (f32[384]{0:T(512)S(1)}, f32[384]{0:T(512)}, u32[]{:S(2)}) copy-start(f32[384]{0:T(512)} %param.11) | copy-start | bytes 4612
  9.4 3.5 %copy-start.6 = (f32[384]{0:T(512)S(1)}, f32[384]{0:T(512)}, u32[]{:S(2)}) copy-start(f32[384]{0:T(512)} %param.10) | copy-start | bytes 4612
  10.9 39.9 %copy-start.1 = (bf16[384,1152]{1,0:T(8,128)(2,1)S(1)}, bf16[384,1152]{1,0:T(8,128)(2,1)}, u32[]{:S(2)}) copy-start(bf16[384,1152]{1,0:T(8,128)(2,1)} %wqkv.1) | copy-start | bytes 2654212
  12.2 38.9 %copy-start.2 = (bf16[384,1536]{1,0:T(8,128)(2,1)S(1)}, bf16[384,1536]{1,0:T(8,128)(2,1)}, u32[]{:S(2)}) copy-start(bf16[384,1536]{1,0:T(8,128)(2,1)} %w1.1) | copy-start | bytes 3538948
  12.2 38.9 %copy-start.4 = (bf16[384,384]{1,0:T(8,128)(2,1)S(1)}, bf16[384,384]{1,0:T(8,128)(2,1)}, u32[]{:S(2)}) copy-start(bf16[384,384]{1,0:T(8,128)(2,1)} %wo.1) | copy-start | bytes 884740
  12.2 38.9 %collective-permute-start = (bf16[4,8,64,384]{3,2,1,0:T(8,128)(2,1)}, bf16[4,8,64,384]{3,2,1,0:T(8,128)(2,1)}, u32[]{:S(2)}, u32[]{:S(2)}) collective-permute-start(bf16[4,8,64,384]{3,2,1,0:T(8,128)(2,1)} %pad_maximum_fusion.1), channel_id=1, source_target_pairs={{0,15},{1,0},{2,1},{3,2},{4,3},{5,4},{6,5},{7,6},{8,7},{9,8},{10,9... | collective-permute-start | bytes 4718600 | tf_op jit(solution)/shard_map/ppermute | solution.py:23
  13.1 0.6 copy-start.5
  51.1 1.3 copy-start.3
  140.8 22.7 %collective-permute-start.2 = (bf16[4,8,64,384]{3,2,1,0:T(8,128)(2,1)}, bf16[4,8,64,384]{3,2,1,0:T(8,128)(2,1)S(1)}, u32[]{:S(2)}, u32[]{:S(2)}) collective-permute-start(bf16[4,8,64,384]{3,2,1,0:T(8,128)(2,1)} %get-tuple-element.7), channel_id=1, source_target_pairs={{0,1},{1,2},{2,3},{3,4},{4,5},{5,6},{6,7},{7,8},{8,9},{9,10},{10,1... | collective-permute-start | bytes 4718600 | tf_op jit(solution)/shard_map/ppermute | solution.py:23

commit v2 on v1

--- a/solution.py
+++ b/solution.py
@@ -33,6 +33,11 @@
 
 def dot_t(a, b):
     return lax.dot_general(a, b, (((1,), (1,)), ((), ())), preferred_element_type=jnp.float32)
+
+
+def row_of(values, row):
+    at = lax.broadcasted_iota(jnp.int32, values.shape, 0)
+    return jnp.sum(jnp.where(at == row, values, 0.0), axis=0, keepdims=True)
 
 
 def strip_kernel(
@@ -117,8 +122,9 @@
             v_aug = jnp.concatenate([v4 * mask, jnp.broadcast_to(mask, (half, 128))], axis=1)
             acc = acc + jnp.dot(p, v_aug, preferred_element_type=jnp.float32)
             peak = jnp.where(mine, m, peak)
-        kcw = kc[0, pl.ds(w, 1), g]
-        vcw = vc[0, pl.ds(w, 1), g]
+        lanes = pl.ds(pl.multiple_of(g * 128, 128), 128)
+        kcw = row_of(kc[:, lanes], 2 * strip + w)
+        vcw = row_of(vc[:, lanes], 2 * strip + w)
         r128 = lax.broadcasted_iota(jnp.int32, (128, 128), 0)
         c128 = lax.broadcasted_iota(jnp.int32, (128, 128), 1)
         k_mat = jnp.where(r128 // HD == c128 // HD, kcw, 0.0).astype(jnp.bfloat16)
@@ -141,7 +147,7 @@
         at = pl.ds(pl.multiple_of(part * tile, tile), tile)
         att = jnp.concatenate([att_s[w, g, at] for g in range(GROUPS)], axis=1)
         mixed = x_s[w, at] + jnp.dot(att, wo[...], preferred_element_type=jnp.float32)
-        mixed = (mixed + delta[0, pl.ds(w, 1)]).astype(jnp.bfloat16).astype(jnp.float32)
+        mixed = (mixed + row_of(delta[...], 2 * strip + w)).astype(jnp.bfloat16).astype(jnp.float32)
         n = norm(mixed, gain2).astype(jnp.bfloat16)
         u = jnp.dot(n, w1[...], preferred_element_type=jnp.float32)
         hidden = 0.5 * u * (1.0 + jnp.tanh((2.0 / jnp.pi) ** 0.5 * (u + 0.044715 * (u * u * u))))
@@ -175,10 +181,6 @@
     def whole(a):
         return pl.BlockSpec(a.shape, lambda b: (0,) * a.ndim)
 
-    per = [
-        pl.BlockSpec((1,) + a.shape[1:], lambda b, n=a.ndim: (b + first,) + (0,) * (n - 1))
-        for a in (delta, kc, vc)
-    ]
     half = WIN**3
     shape = jax.ShapeDtypeStruct((HALF, 2 * count, HALF * 16, C), jnp.bfloat16)
     out_spec = pl.BlockSpec(shape.shape, lambda b: (0, 0, 0, 0))
@@ -196,8 +198,7 @@
             whole(g1),
             whole(g2),
         ]
-        + [whole(w) for w in ws]
-        + per,
+        + [whole(w) for w in (*ws, delta, kc, vc)],
         out_specs=(out_spec, out_spec),
         scratch_shapes=[
             pltpu.VMEM((2, half, C), jnp.float32),
@@ -217,39 +218,140 @@
     )(last, volume, volume, halo, halo, g1, g2, *ws, delta, kc, vc)
 
 
-def carriers(volume, g1, wc, wco, wr):
+def sums_kernel(volume, out):
+    planes = volume.shape[0]
+    block = volume[:, 0].astype(jnp.float32)
+    out[0] = block.reshape(planes // HALF, HALF * HALF, 16, C).sum(axis=1)
+
+
+def half_sums(volume):
     planes, yh = volume.shape[:2]
+    return pl.pallas_call(
+        sums_kernel,
+        grid=(yh,),
+        out_shape=jax.ShapeDtypeStruct((yh, planes // HALF, 16, C), jnp.float32),
+        in_specs=[pl.BlockSpec((planes, 1, HALF * 16, C), lambda y: (0, y, 0, 0))],
+        out_specs=pl.BlockSpec((1, planes // HALF, 16, C), lambda y: (y, 0, 0, 0)),
+        cost_estimate=pl.CostEstimate(
+            flops=2 * volume.size, bytes_accessed=2 * volume.size, transcendentals=0
+        ),
+        name="half_sums",
+    )(volume)
+
+
+def carrier_kernel(
+    n, parts, g1, wc, wco, wr, delta_out, kc_out, vc_out,
+    sums, arrived, everyone, halo_send, halo_recv, send_sem, recv_sem,
+):
+    me = lax.axis_index("slab")
+    barrier = pltpu.get_barrier_semaphore()
+
+    @pl.loop(1, n)
+    def _(d):
+        pl.semaphore_signal(
+            barrier, inc=1, device_id={"slab": lax.rem(me + d, n)}, device_id_type=pl.DeviceIdType.MESH
+        )
+
+    yh = parts.shape[0]
     strips = yh // 2
-    parts = volume.astype(jnp.float32).reshape(2, HALF, yh, HALF, 16, C).sum(axis=(1, 3))
-    inner = parts[:, :, 4:12].sum(axis=2)
-    outer = parts[:, :, :4].sum(axis=2) + parts[:, :, 12:].sum(axis=2)
-    sums = jnp.stack([inner, outer], axis=2)
-    sums = jnp.roll(sums, -1, axis=1).reshape(2, strips, 2, 2, C).sum(axis=2)
-    sums = sums.reshape(2, strips * 2, C)
-    arrived = shifted(sums[0], "slab", -1)
-    carrier = (sums[1] + arrived) * (1.0 / WIN**3)
+    for b in range(strips):
+        both = parts[2 * b + 1] + parts[(2 * b + 2) % yh]
+        for z in range(2):
+            inner = both[z, 4:12].sum(axis=0, keepdims=True)
+            outer = both[z].sum(axis=0, keepdims=True) - inner
+            sums[z, 2 * b : 2 * b + 1] = inner
+            sums[z, 2 * b + 1 : 2 * b + 2] = outer
+    pl.semaphore_wait(barrier, n - 1)
+    copy = pltpu.make_async_remote_copy(
+        src_ref=sums.at[0],
+        dst_ref=arrived,
+        send_sem=halo_send,
+        recv_sem=halo_recv,
+        device_id={"slab": lax.rem(me + n - 1, n)},
+        device_id_type=pl.DeviceIdType.MESH,
+    )
+    copy.start()
+    copy.wait()
+    gain = g1[...]
+    carrier = (sums[1] + arrived[...]) * (1.0 / WIN**3)
     count = carrier.shape[0]
-    normed = norm(carrier, g1).astype(jnp.bfloat16)
-    proj = jnp.dot(normed, wc, preferred_element_type=jnp.float32).astype(jnp.bfloat16)
-    asking = proj[:, :C].reshape(count, HEADS, HD)
-    everyone = lax.all_gather(proj[:, C:], "slab", axis=0, tiled=True)
-    keys = everyone[:, :C].reshape(-1, HEADS, HD)
-    values = everyone[:, C:].reshape(-1, HEADS, HD).astype(jnp.float32)
-    s = jnp.einsum("chd,rhd->hcr", asking, keys, preferred_element_type=jnp.float32) * HD**-0.5
-    weights = jax.nn.softmax(s, axis=-1)
-    mix = jnp.einsum("hcr,rhd->chd", weights, values, precision=lax.Precision.HIGHEST)
-    mix = mix.reshape(count, C).astype(jnp.bfloat16)
-    delta = jnp.dot(mix, wco, preferred_element_type=jnp.float32)
-    kv = jnp.dot(
-        norm(carrier + delta, g1).astype(jnp.bfloat16), wr[:, C:], preferred_element_type=jnp.float32
+    normed = norm(carrier, gain).astype(jnp.bfloat16)
+    proj = jnp.dot(normed, wc[...], preferred_element_type=jnp.float32)
+    proj = proj.astype(jnp.bfloat16).astype(jnp.float32)
+    everyone[me] = proj[:, C:]
+
+    def peer(d):
+        return pltpu.make_async_remote_copy(
+            src_ref=everyone.at[me],
+            dst_ref=everyone.at[me],
+            send_sem=send_sem.at[d],
+            recv_sem=recv_sem.at[d],
+            device_id={"slab": lax.rem(me + d, n)},
+            device_id_type=pl.DeviceIdType.MESH,
+        )
+
+    @pl.loop(1, n)
+    def _(d):
+        peer(d).start()
+
+    @pl.loop(1, n)
+    def _(d):
+        peer(d).wait()
+
+    kv = everyone[...].reshape(n * count, 2 * C).astype(jnp.bfloat16)
+    lane = lax.broadcasted_iota(jnp.int32, (count, C), 1) // HD
+    asking = jnp.concatenate(
+        [jnp.where(lane == h, proj[:, :C], 0.0) for h in range(HEADS)], axis=0
     ).astype(jnp.bfloat16)
-    kv = kv.astype(jnp.float32)
-    kc = kv[:, :C].reshape(strips, 2, GROUPS, 128)
-    vc = kv[:, C:].reshape(strips, 2, GROUPS, 128)
-    return delta.reshape(strips, 2, C), kc, vc
-
-
-CALLS = 1
+    s = dot_t(asking, kv[:, :C]) * HD**-0.5
+    p = jnp.exp(s - jnp.max(s, axis=1, keepdims=True))
+    p = p / jnp.sum(p, axis=1, keepdims=True)
+    high = p.astype(jnp.bfloat16)
+    low = (p - high.astype(jnp.float32)).astype(jnp.bfloat16)
+    wide = jnp.dot(high, kv[:, C:], preferred_element_type=jnp.float32) + jnp.dot(
+        low, kv[:, C:], preferred_element_type=jnp.float32
+    )
+    mix = jnp.zeros((count, C), jnp.float32)
+    for h in range(HEADS):
+        mix = jnp.where(lane == h, wide[h * count : (h + 1) * count], mix)
+    delta = jnp.dot(mix.astype(jnp.bfloat16), wco[...], preferred_element_type=jnp.float32)
+    delta_out[...] = delta
+    own = jnp.dot(
+        norm(carrier + delta, gain).astype(jnp.bfloat16),
+        wr[:, C:],
+        preferred_element_type=jnp.float32,
+    )
+    own = own.astype(jnp.bfloat16).astype(jnp.float32)
+    kc_out[...] = own[:, :C]
+    vc_out[...] = own[:, C:]
+
+
+def carriers(parts, g1, wc, wco, wr):
+    n = lax.axis_size("slab")
+    count = parts.shape[0]
+    shape = jax.ShapeDtypeStruct((count, C), jnp.float32)
+    return pl.pallas_call(
+        functools.partial(carrier_kernel, n),
+        out_shape=(shape,) * 3,
+        in_specs=[pl.BlockSpec(memory_space=pltpu.VMEM)] * 5,
+        out_specs=(pl.BlockSpec(memory_space=pltpu.VMEM),) * 3,
+        scratch_shapes=[
+            pltpu.VMEM((2, count, C), jnp.float32),
+            pltpu.VMEM((count, C), jnp.float32),
+            pltpu.VMEM((n, count, 2 * C), jnp.float32),
+            pltpu.SemaphoreType.DMA,
+            pltpu.SemaphoreType.DMA,
+            pltpu.SemaphoreType.DMA((n,)),
+            pltpu.SemaphoreType.DMA((n,)),
+        ],
+        compiler_params=pltpu.CompilerParams(
+            collective_id=0, has_side_effects=True, vmem_limit_bytes=24 * 1024 * 1024
+        ),
+        cost_estimate=pl.CostEstimate(
+            flops=10**9, bytes_accessed=30 * 10**6, transcendentals=20000
+        ),
+        name="carriers",
+    )(parts, g1, wc, wco, wr)
 
 
 def body(volume_features, g1, g2, wc, wco, wr, wro, w1, w2):
@@ -259,23 +361,29 @@
     volume = volume_features.reshape(planes, yh, HALF * nx, channels)
     position = lax.axis_index("slab")
     last = (position == lax.axis_size("slab") - 1).astype(jnp.int32).reshape(1)
-    sent = jnp.concatenate([volume[:HALF, 1:], volume[:HALF, :1]], axis=1)
-    per = strips // CALLS
-    halos = [shifted(sent[:, 2 * per * i : 2 * per * (i + 1)], "slab", -1) for i in range(CALLS)]
-    delta, kc, vc = carriers(volume, g1, wc, wco, wr)
+    cuts = [(0, strips - 1), (strips - 1, strips)]
+    halos = []
+    for lo, hi in cuts:
+        if hi < strips:
+            sent = volume[:HALF, 2 * lo + 1 : 2 * hi + 1]
+        else:
+            sent = jnp.concatenate([volume[:HALF, 2 * lo + 1 :], volume[:HALF, :1]], axis=1)
+        halos.append(shifted(sent, "slab", -1))
     gains = (g1.reshape(1, channels), g2.reshape(1, channels))
+    delta, kc, vc = carriers(half_sums(volume), gains[0], wc, wco, wr)
     ws = (wr, wro, w1, w2)
     local, returned = [], []
-    for i in range(CALLS):
+    for (lo, hi), halo in zip(cuts, halos):
         out_loc, out_halo = strips_call(
-            i * per, per, strips, last, volume, halos[i], 0, *gains, ws, delta, kc, vc
+            lo, hi - lo, strips, last, volume, halo, 0, *gains, ws, delta, kc, vc
         )
         local.append(out_loc)
         returned.append(shifted(out_halo, "slab", 1))
-    local = jnp.concatenate(local, axis=1)
-    returned = jnp.concatenate(returned, axis=1)
+    local = jnp.concatenate([local[-1][:, -1:]] + local[:-1] + [local[-1][:, :-1]], axis=1)
+    returned = jnp.concatenate(
+        [returned[-1][:, -1:]] + returned[:-1] + [returned[-1][:, :-1]], axis=1
+    )
     done = jnp.concatenate([returned, local], axis=0)
-    done = jnp.concatenate([done[:, -1:], done[:, :-1]], axis=1)
     return done.reshape(volume_features.shape)
 
 

time: 167 us -> 138 us (0.83)
  blocking collectives: 32.8 us -> 0 us
  Pallas kernels: 88.4 us -> 112 us
  waiting for transfers between devices: 22.4 us -> 9.24 us
  other arithmetic: 6.84 us -> 2.74 us
  matrix products: 3.03 us -> 0 us
    all_gather x1 -> x0, blocking collectives: 32.8 us -> none  [carriers(): everyone = lax.all_gather(proj[:, C:], 'slab', axis=0, tiled=True)]
    pallas_call x0 -> x2, Pallas kernels: none -> 22.9 us  [the longest x1 17.2 us: carriers(): pl.pallas_call(functools.partial(carrier_kernel, n), out_shape=(shape,) *...]
    ppermute x3 -> x4, waiting for transfers between devices: 22.4 us -> 9.24 us  [shifted(): return lax.ppermute(value, axis, pairs)]
    reduce_sum x8 -> x0, other arithmetic: 3.45 us -> none  [the longest x1 2.53 us: carriers(): volume.astype(jnp.float32).reshape(2, HALF, yh, HALF, 16, C)]
    dot_general x5 -> x0, matrix products: 3.03 us -> none  [the longest x1 1.23 us: carriers(): delta = jnp.dot(mix, wco, preferred_element_type=jnp.float32)]
    ppermute x3 -> x4, starting transfers between devices: 6.51 us -> 7.58 us  [shifted(): return lax.ppermute(value, axis, pairs)]
    concatenate x3 -> x2, other arithmetic: 3.35 us -> 2.74 us  [the longest x1 1.95 us: body(): done = jnp.concatenate([returned, local], axis=0)]
    slice x12 -> x4, local copies, waits for them, and re-layouts: 3.11 us -> 3.59 us  [the longest x1 2.45 us: body(): sent = volume[:HALF, 2 * lo + 1:2 * hi + 1]]
  transfers between devices with their start and end apart: 3 -> 4, of which waited for: 1 -> 1; matrix products, arithmetic and copies ran while one was open for 5% -> 1% of each run, Pallas kernels for 0% -> 81%
where the time goes in v2:
time: 138 us; the launch traced here: 137 us
  Pallas kernels  112 us (81%)
  waiting for transfers between devices  9.24 us (7%)
  starting transfers between devices  7.58 us (5%)
  local copies, waits for them, and re-layouts  5.79 us (4%)
  other arithmetic  2.74 us (2%)
    pallas_call x2, Pallas kernels, strips_call(): pl.pallas_call(functools.partial(strip_kernel, first, strips), grid=(coun...  88.8 us
    pallas_call x1, Pallas kernels, carriers(): pl.pallas_call(functools.partial(carrier_kernel, n), out_shape=(shape,) *...  17.2 us
    ppermute x4, waiting for transfers between devices, shifted(): return lax.ppermute(value, axis, pairs)  9.24 us
    ppermute x4, starting transfers between devices, shifted(): return lax.ppermute(value, axis, pairs)  7.58 us
    pallas_call x1, Pallas kernels, half_sums(): pl.pallas_call(sums_kernel, grid=(yh,), out_shape=jax.ShapeDtypeStruct((y...  5.7 us
  transfers between devices with their start and end apart: 4, of which 1 were waited for; matrix products, arithmetic and copies ran while one was open for 1% of the time, Pallas kernels for 81%

profile of v2, /device:TPU:0, one launch (start us, length us, event | category | flops | bytes accessed | tf_op | source)
XLA Modules:
  0.0 137.2 jit_solution(13899646614823323800)
XLA Ops:
  0.0 0.0 copy-start.8
  0.0 0.0 copy-start.9
  0.0 2.4 %slice.31 = bf16[4,6,64,384]{3,2,1,0:T(8,128)(2,1)} slice(bf16[8,8,64,384]{3,2,1,0:T(8,128)(2,1)} %bitcast.3), slice={[0:4], [1:7], [0:64], [0:384]} | slice | bytes 2359296 | tf_op jit(solution)/shard_map/slice | solution.py:368
  2.5 0.0 copy-start.3
  2.5 0.0 copy-start.6
  2.5 5.4 %collective-permute-start.2 = (bf16[4,6,64,384]{3,2,1,0:T(8,128)(2,1)}, bf16[4,6,64,384]{3,2,1,0:T(8,128)(2,1)S(1)}, u32[]{:S(2)}, u32[]{:S(2)}) collective-permute-start(bf16[4,6,64,384]{3,2,1,0:T(8,128)(2,1)} %slice.31), channel_id=1, source_target_pairs={{0,15},{1,0},{2,1},{3,2},{4,3},{5,4},{6,5},{7,6},{8,7},{9,8},{10,9... | collective-permute-start | bytes 3538952 | tf_op jit(solution)/shard_map/ppermute | solution.py:23
  7.9 1.1 fusion
  9.0 0.8 pad_maximum_fusion
  9.8 0.7 collective-permute-start
  10.4 0.0 copy-done.8
  10.4 0.0 copy-done.9
  10.4 0.0 copy-start.1
  10.5 5.7 %half_sums.1.parts = f32[8,2,16,384]{3,2,1,0:T(8,128)} custom-call(bf16[8,8,64,384]{3,2,1,0:T(8,128)(2,1)} %bitcast.5), custom_call_target="tpu_custom_call" | custom-call | flops 3145728 | bytes 3145728 | tf_op jit(solution)/shard_map/half_sums/pallas_call | solution.py:229
  16.2 0.0 copy-done.3
  16.2 0.0 copy-done.6
  16.2 0.0 copy-start
  16.2 1.0 copy-done
  17.2 0.0 copy-start.4
  17.2 1.2 copy-done.4
  18.3 0.0 copy-start.5
  18.3 0.0 copy-start.7
  18.3 17.2 %carriers.1 = (f32[8,384]{1,0:T(8,128)S(1)}, f32[8,384]{1,0:T(8,128)S(1)}, f32[8,384]{1,0:T(8,128)S(1)}) custom-call(f32[8,2,16,384]{3,2,1,0:T(8,128)S(1)} %copy-done, f32[1,384]{1,0:T(1,128)S(1)} %reshape.20.g1, bf16[384,1152]{1,0:T(8,128)(2,1)S(1)} %copy-done.3, bf16[384,384]{1,0:T(8,128)(2,1)S(1)} %copy-done.6, bf16[384,1152]{1,0:T(8,128)(2,1)S(1)} %copy-done.4), custom_call_target="tpu_custom_call" | custom-call | flops 1000000000 | bytes 30000000 | tf_op jit(solution)/shard_map/carriers/pallas_call | solution.py:333
  35.6 0.0 collective-permute-done.2.halo_a.halo_b
  35.6 0.0 copy-done.1
  35.6 0.0 copy-done.5
  35.6 0.0 copy-done.7
  35.6 0.0 copy-start.2
  35.6 66.2 %strips.3 = (bf16[4,6,64,384]{3,2,1,0:T(8,128)(2,1)S(1)}, bf16[4,6,64,384]{3,2,1,0:T(8,128)(2,1)S(1)}) custom-call(s32[1]{0:T(128)} %bitcast.last_ref, bf16[8,8,64,384]{3,2,1,0:T(8,128)(2,1)} %bitcast.6, bf16[8,8,64,384]{3,2,1,0:T(8,128)(2,1)} %bitcast.7, bf16[4,6,64,384]{3,2,1,0:T(8,128)(2,1)S(1)} %collective-permute-done.2.halo_a.halo_b, ...), custom_call_target="tpu_custom_call" | custom-call | flops 22951231488 | bytes 9437184 | tf_op jit(solution)/shard_map/strips/pallas_call | solution.py:188
  101.8 0.3 collective-permute-start.3
  102.1 0.0 collective-permute-done.halo_a.halo_b
  102.1 0.0 copy-done.2
  102.1 22.6 %strips.2 = (bf16[4,2,64,384]{3,2,1,0:T(8,128)(2,1)S(1)}, bf16[4,2,64,384]{3,2,1,0:T(8,128)(2,1)S(1)}) custom-call(s32[1]{0:T(128)} %bitcast.last_ref, bf16[8,8,64,384]{3,2,1,0:T(8,128)(2,1)} %bitcast.8, bf16[8,8,64,384]{3,2,1,0:T(8,128)(2,1)} %bitcast.9, bf16[4,2,64,384]{3,2,1,0:T(8,128)(2,1)} %collective-permute-done.halo_a.halo_b, ...), custom_call_target="tpu_custom_call" | custom-call | flops 7650410496 | bytes 3145728 | tf_op jit(solution)/shard_map/strips/pallas_call | solution.py:188
  124.8 1.2 collective-permute-start.1
  126.0 9.2 %collective-permute-done.1 = bf16[4,2,64,384]{3,2,1,0:T(8,128)(2,1)S(1)} collective-permute-done((bf16[4,2,64,384]{3,2,1,0:T(8,128)(2,1)S(1)}, bf16[4,2,64,384]{3,2,1,0:T(8,128)(2,1)S(1)}, u32[]{:S(2)}, u32[]{:S(2)}) %collective-permute-start.1) | collective-permute-done | bytes 393248 | tf_op jit(solution)/shard_map/ppermute | solution.py:23
  135.3 0.0 collective-permute-done.3
  135.3 1.9 %maximum_maximum_fusion = bf16[8,8,64,384]{3,2,1,0:T(8,128)(2,1)} fusion(bf16[4,1,64,384]{3,2,1,0:T(8,128)(2,1)S(1)} %get-tuple-element.24, bf16[4,6,64,384]{3,2,1,0:T(8,128)(2,1)S(1)} %get-tuple-element.18, bf16[4,1,64,384]{3,2,1,0:T(8,128)(2,1)S(1)} %get-tuple-element.23, bf16[4,1,64,384]{3,2,1,0:T(8,128)(2,1)S(1)} %get-tuple-element.22, ...), kind=kLoop, calls=%fused_computation | loop fusion | flops 7864320 | bytes 6291456 | tf_op jit(solution)/shard_map/concatenate | solution.py:386
  (4 shorter events, 0.1 us)
Async XLA Ops:
  0.0 10.4 %copy-start.8 = (f32[384]{0:T(512)S(1)}, f32[384]{0:T(512)}, u32[]{:S(2)}) copy-start(f32[384]{0:T(512)} %param.10) | copy-start | bytes 4612
  0.0 10.4 %copy-start.9 = (f32[384]{0:T(512)S(1)}, f32[384]{0:T(512)}, u32[]{:S(2)}) copy-start(f32[384]{0:T(512)} %param.11) | copy-start | bytes 4612
  2.5 13.7 %copy-start.3 = (bf16[384,1152]{1,0:T(8,128)(2,1)S(1)}, bf16[384,1152]{1,0:T(8,128)(2,1)}, u32[]{:S(2)}) copy-start(bf16[384,1152]{1,0:T(8,128)(2,1)} %wc.1) | copy-start | bytes 2654212
  2.5 13.7 %copy-start.6 = (bf16[384,384]{1,0:T(8,128)(2,1)S(1)}, bf16[384,384]{1,0:T(8,128)(2,1)}, u32[]{:S(2)}) copy-start(bf16[384,384]{1,0:T(8,128)(2,1)} %wco.1) | copy-start | bytes 884740
  2.5 33.1 %collective-permute-start.2 = (bf16[4,6,64,384]{3,2,1,0:T(8,128)(2,1)}, bf16[4,6,64,384]{3,2,1,0:T(8,128)(2,1)S(1)}, u32[]{:S(2)}, u32[]{:S(2)}) collective-permute-start(bf16[4,6,64,384]{3,2,1,0:T(8,128)(2,1)} %slice.31), channel_id=1, source_target_pairs={{0,15},{1,0},{2,1},{3,2},{4,3},{5,4},{6,5},{7,6},{8,7},{9,8},{10,9... | collective-permute-start | bytes 3538952 | tf_op jit(solution)/shard_map/ppermute | solution.py:23
  9.8 92.4 %collective-permute-start = (bf16[4,2,64,384]{3,2,1,0:T(8,128)(2,1)}, bf16[4,2,64,384]{3,2,1,0:T(8,128)(2,1)}, u32[]{:S(2)}, u32[]{:S(2)}) collective-permute-start(bf16[4,2,64,384]{3,2,1,0:T(8,128)(2,1)} %pad_maximum_fusion), channel_id=1, source_target_pairs={{0,15},{1,0},{2,1},{3,2},{4,3},{5,4},{6,5},{7,6},{8,7},{9,8},{10,9... | collective-permute-start | bytes 1179656 | tf_op jit(solution)/shard_map/ppermute | solution.py:23
  10.4 25.1 %copy-start.1 = (bf16[384,1536]{1,0:T(8,128)(2,1)S(1)}, bf16[384,1536]{1,0:T(8,128)(2,1)}, u32[]{:S(2)}) copy-start(bf16[384,1536]{1,0:T(8,128)(2,1)} %w1.3) | copy-start | bytes 3538948
  16.2 1.0 copy-start
  17.2 1.2 copy-start.4
  18.3 17.2 %copy-start.5 = (bf16[384,1152]{1,0:T(8,128)(2,1)S(1)}, bf16[384,1152]{1,0:T(8,128)(2,1)}, u32[]{:S(2)}) copy-start(bf16[384,1152]{1,0:T(8,128)(2,1)} %wqkv.3) | copy-start | bytes 2654212
  18.3 17.3 %copy-start.7 = (bf16[384,384]{1,0:T(8,128)(2,1)S(1)}, bf16[384,384]{1,0:T(8,128)(2,1)}, u32[]{:S(2)}) copy-start(bf16[384,384]{1,0:T(8,128)(2,1)} %wo.3) | copy-start | bytes 884740
  35.6 66.5 %copy-start.2 = (bf16[1536,384]{1,0:T(8,128)(2,1)S(1)}, bf16[1536,384]{1,0:T(8,128)(2,1)}, u32[]{:S(2)}) copy-start(bf16[1536,384]{1,0:T(8,128)(2,1)} %w2.3) | copy-start | bytes 3538948
  101.8 33.4 %collective-permute-start.3 = (bf16[4,6,64,384]{3,2,1,0:T(8,128)(2,1)S(1)}, bf16[4,6,64,384]{3,2,1,0:T(8,128)(2,1)S(1)}, u32[]{:S(2)}, u32[]{:S(2)}) collective-permute-start(bf16[4,6,64,384]{3,2,1,0:T(8,128)(2,1)S(1)} %get-tuple-element.16), channel_id=1, source_target_pairs={{0,1},{1,2},{2,3},{3,4},{4,5},{5,6},{6,7},{7,8},{8,9},{9,10},{10,1... | collective-permute-start | bytes 3538952 | tf_op jit(solution)/shard_map/ppermute | solution.py:23
  124.8 10.4 %collective-permute-start.1 = (bf16[4,2,64,384]{3,2,1,0:T(8,128)(2,1)S(1)}, bf16[4,2,64,384]{3,2,1,0:T(8,128)(2,1)S(1)}, u32[]{:S(2)}, u32[]{:S(2)}) collective-permute-start(bf16[4,2,64,384]{3,2,1,0:T(8,128)(2,1)S(1)} %get-tuple-element.15), channel_id=1, source_target_pairs={{0,1},{1,2},{2,3},{3,4},{4,5},{5,6},{6,7},{7,8},{8,9},{9,10},{10,1... | collective-permute-start | bytes 1179656 | tf_op jit(solution)/shard_map/ppermute | solution.py:23

commit v3 on v2

--- a/solution.py
+++ b/solution.py
@@ -54,6 +54,7 @@
     wo,
     w1,
     w2,
+    wvt,
     delta,
     kc,
     vc,
@@ -61,6 +62,7 @@
     out_halo,
     x_s,
     qkv_s,
+    vt_s,
     att_s,
     y_s,
 ):
@@ -77,7 +79,10 @@
         x_w = tokens[:, w].reshape(half, C)
         x_s[w] = x_w
         n_w = norm(x_w, gain1).astype(jnp.bfloat16)
-        for part in range(3):
+        vt = dot_t(wvt[...], n_w).astype(jnp.bfloat16)
+        for g in range(GROUPS):
+            vt_s[w, g] = vt[g * 128 : (g + 1) * 128]
+        for part in range(2):
             proj = jnp.dot(
                 n_w, wqkv[:, part * C : (part + 1) * C], preferred_element_type=jnp.float32
             )
@@ -106,37 +111,36 @@
         feat_q = jnp.where(same, 0.0, -BIG).astype(jnp.bfloat16)
         feat_k = jnp.where(same, 1.0, 0.0).astype(jnp.bfloat16)
         q4 = qkv_s[0, w, g]
-        k4 = qkv_s[1, w, g]
-        v4 = qkv_s[2, w, g]
-        k_aug = jnp.concatenate([k4, feat_k], axis=1)
-        acc = jnp.zeros((half, 256), jnp.float32)
-        peak = jnp.zeros((half, 128), jnp.float32)
-        zero = jnp.zeros((), jnp.bfloat16)
-        for h in range(4):
-            mine = (lane // HD) == h
-            mask = jnp.where(mine, 1.0, 0.0).astype(jnp.bfloat16)
-            q_aug = jnp.concatenate([q4 * mask, feat_q], axis=1)
-            s = dot_t(q_aug, k_aug)
-            m = jnp.max(s, axis=1, keepdims=True)
-            p = jnp.exp2(s - m).astype(jnp.bfloat16)
-            v_aug = jnp.concatenate([v4 * mask, jnp.broadcast_to(mask, (half, 128))], axis=1)
-            acc = acc + jnp.dot(p, v_aug, preferred_element_type=jnp.float32)
-            peak = jnp.where(mine, m, peak)
+        vt4 = vt_s[w, g]
+        k_aug = jnp.concatenate([qkv_s[1, w, g], feat_k], axis=1)
         lanes = pl.ds(pl.multiple_of(g * 128, 128), 128)
         kcw = row_of(kc[:, lanes], 2 * strip + w)
         vcw = row_of(vc[:, lanes], 2 * strip + w)
+        r16 = lax.broadcasted_iota(jnp.int32, (16, 128), 0)
+        k_rows = jnp.where(lane // HD == r16, kcw, 0.0).astype(jnp.bfloat16)
+        affinity = dot_t(k_rows, q4)
         r128 = lax.broadcasted_iota(jnp.int32, (128, 128), 0)
-        c128 = lax.broadcasted_iota(jnp.int32, (128, 128), 1)
-        k_mat = jnp.where(r128 // HD == c128 // HD, kcw, 0.0).astype(jnp.bfloat16)
-        c4 = dot_t(q4, k_mat)
-        top = jnp.maximum(peak, c4)
-        a = jnp.exp2(peak - top)
-        e = jnp.exp2(c4 - top)
-        att = (acc[:, :128] * a + e * vcw) / (acc[:, 128:] * a + e)
-        att_s[w, g] = att.astype(jnp.bfloat16)
+        v_col = jnp.sum(jnp.where(r128 == lane, vcw, 0.0), axis=1, keepdims=True)
+        ones = jnp.ones((16, half), jnp.bfloat16)
+        blocks = []
+        for h in range(4):
+            mask = jnp.where((lane // HD) == h, 1.0, 0.0).astype(jnp.bfloat16)
+            q_aug = jnp.concatenate([q4 * mask, feat_q], axis=1)
+            s = dot_t(k_aug, q_aug)
+            m = jnp.max(s, axis=0, keepdims=True)
+            p = jnp.exp2(s - m).astype(jnp.bfloat16)
+            own = slice(h * HD, (h + 1) * HD)
+            vt = jnp.concatenate([vt4[own], ones], axis=0)
+            o = jnp.dot(vt, p, preferred_element_type=jnp.float32)
+            c = affinity[h : h + 1]
+            top = jnp.maximum(m, c)
+            a = jnp.exp2(m - top)
+            e = jnp.exp2(c - top)
+            blocks.append((o[:HD] * a + e * v_col[own]) / (o[HD : HD + 1] * a + e))
+        att_s[w, g] = jnp.concatenate(blocks, axis=0).T.astype(jnp.bfloat16)
         return carry
 
-    lax.fori_loop(0, 2 * GROUPS, attend, 0)
+    lax.fori_loop(0, 2 * GROUPS, attend, 0, unroll=3)
 
     gain2 = g2[...]
     tile = half // 2
@@ -202,7 +206,8 @@
         out_specs=(out_spec, out_spec),
         scratch_shapes=[
             pltpu.VMEM((2, half, C), jnp.float32),
-            pltpu.VMEM((3, 2, GROUPS, half, 128), jnp.bfloat16),
+            pltpu.VMEM((2, 2, GROUPS, half, 128), jnp.bfloat16),
+            pltpu.VMEM((2, GROUPS, 128, half), jnp.bfloat16),
             pltpu.VMEM((2, GROUPS, half, 128), jnp.bfloat16),
             pltpu.VMEM((2 * half // 16, 2, 8, C), jnp.float32),
         ],
@@ -371,7 +376,7 @@
         halos.append(shifted(sent, "slab", -1))
     gains = (g1.reshape(1, channels), g2.reshape(1, channels))
     delta, kc, vc = carriers(half_sums(volume), gains[0], wc, wco, wr)
-    ws = (wr, wro, w1, w2)
+    ws = (wr, wro, w1, w2, wr[:, 2 * channels :].T)
     local, returned = [], []
     for (lo, hi), halo in zip(cuts, halos):
         out_loc, out_halo = strips_call(

time: 138 us -> 143 us (1.036)
  Pallas kernels: 112 us -> 118 us
    pallas_call x2, Pallas kernels: 88.8 us -> 94.3 us  [strips_call(): pl.pallas_call(functools.partial(strip_kernel, first, strips), grid=(coun...]
  transfers between devices with their start and end apart: 4 -> 4, of which waited for: 1 -> 1; matrix products, arithmetic and copies ran while one was open for 1% -> 2% of each run, Pallas kernels for 81% -> 83%
where the time goes in v3:
time: 143 us
  Pallas kernels  118 us (83%)
  waiting for transfers between devices  9.25 us (6%)
  starting transfers between devices  7.6 us (5%)
  local copies, waits for them, and re-layouts  4.86 us (3%)
  other arithmetic  2.75 us (2%)
    pallas_call x2, Pallas kernels, strips_call(): pl.pallas_call(functools.partial(strip_kernel, first, strips), grid=(coun...  94.3 us
    pallas_call x1, Pallas kernels, carriers(): pl.pallas_call(functools.partial(carrier_kernel, n), out_shape=(shape,) *...  18.2 us
    ppermute x4, waiting for transfers between devices, shifted(): return lax.ppermute(value, axis, pairs)  9.25 us
    ppermute x4, starting transfers between devices, shifted(): return lax.ppermute(value, axis, pairs)  7.6 us
    pallas_call x1, Pallas kernels, half_sums(): pl.pallas_call(sums_kernel, grid=(yh,), out_shape=jax.ShapeDtypeStruct((y...  5.65 us
  transfers between devices with their start and end apart: 4, of which 1 were waited for; matrix products, arithmetic and copies ran while one was open for 2% of the time, Pallas kernels for 83%

profile of v3, /device:TPU:0, one launch (start us, length us, event | category | flops | bytes accessed | tf_op | source)
XLA Modules:
  0.0 142.7 jit_solution(797761138000301534)
XLA Ops:
  0.0 0.0 copy-start.7
  0.0 0.0 copy-start.8
  0.0 0.0 slice-start
  0.0 2.5 %slice.35 = bf16[4,6,64,384]{3,2,1,0:T(8,128)(2,1)} slice(bf16[8,8,64,384]{3,2,1,0:T(8,128)(2,1)} %bitcast.6), slice={[0:4], [1:7], [0:64], [0:384]} | slice | bytes 2359296 | tf_op jit(solution)/shard_map/slice | solution.py:373
  2.5 0.0 copy-start.1
  2.5 0.0 copy-start.4
  2.5 5.5 %collective-permute-start.2 = (bf16[4,6,64,384]{3,2,1,0:T(8,128)(2,1)}, bf16[4,6,64,384]{3,2,1,0:T(8,128)(2,1)S(1)}, u32[]{:S(2)}, u32[]{:S(2)}) collective-permute-start(bf16[4,6,64,384]{3,2,1,0:T(8,128)(2,1)} %slice.35), channel_id=1, source_target_pairs={{0,15},{1,0},{2,1},{3,2},{4,3},{5,4},{6,5},{7,6},{8,7},{9,8},{10,9... | collective-permute-start | bytes 3538952 | tf_op jit(solution)/shard_map/ppermute | solution.py:23
  7.9 1.1 fusion
  9.0 0.8 pad_maximum_fusion
  9.8 0.7 collective-permute-start
  10.5 0.0 copy-done.7
  10.5 0.0 copy-done.8
  10.5 0.0 slice-done
  10.5 0.2 copy.11
  10.7 0.0 copy-start.5
  10.7 5.7 %half_sums.1.parts = f32[8,2,16,384]{3,2,1,0:T(8,128)} custom-call(bf16[8,8,64,384]{3,2,1,0:T(8,128)(2,1)} %bitcast.8), custom_call_target="tpu_custom_call" | custom-call | flops 3145728 | bytes 3145728 | tf_op jit(solution)/shard_map/half_sums/pallas_call | solution.py:234
  16.4 0.0 copy-done.1
  16.4 0.0 copy-done.4
  16.4 0.0 copy-done.5
  16.4 0.0 copy-start
  16.4 1.0 copy-done
  17.4 0.0 copy-start.6
  17.4 18.2 %carriers.1 = (f32[8,384]{1,0:T(8,128)S(1)}, f32[8,384]{1,0:T(8,128)S(1)}, f32[8,384]{1,0:T(8,128)S(1)}) custom-call(f32[8,2,16,384]{3,2,1,0:T(8,128)S(1)} %copy-done, f32[1,384]{1,0:T(1,128)S(1)} %reshape.20.g1, bf16[384,1152]{1,0:T(8,128)(2,1)S(1)} %copy-done.4, bf16[384,384]{1,0:T(8,128)(2,1)S(1)} %copy-done.5, bf16[384,1152]{1,0:T(8,128)(2,1)S(1)} %copy-done.1), custom_call_target="tpu_custom_call" | custom-call | flops 1000000000 | bytes 30000000 | tf_op jit(solution)/shard_map/carriers/pallas_call | solution.py:338
  35.6 0.0 collective-permute-done.2.halo_a.halo_b
  35.6 0.0 copy-done.6
  35.6 0.0 copy-start.2
  35.6 0.0 copy-start.3
  35.6 70.4 %strips.3 = (bf16[4,6,64,384]{3,2,1,0:T(8,128)(2,1)S(1)}, bf16[4,6,64,384]{3,2,1,0:T(8,128)(2,1)S(1)}) custom-call(s32[1]{0:T(128)} %bitcast.last_ref, bf16[8,8,64,384]{3,2,1,0:T(8,128)(2,1)} %bitcast.9, bf16[8,8,64,384]{3,2,1,0:T(8,128)(2,1)} %bitcast.10, bf16[4,6,64,384]{3,2,1,0:T(8,128)(2,1)S(1)} %collective-permute-done.2.halo_a.halo_b, ...), custom_call_target="tpu_custom_call" | custom-call | flops 22951231488 | bytes 9437184 | tf_op jit(solution)/shard_map/strips/pallas_call | solution.py:192
  106.0 0.3 collective-permute-start.3
  106.3 0.0 collective-permute-done.halo_a.halo_b
  106.3 0.0 copy-done.2
  106.3 0.0 copy-done.3
  106.3 23.9 %strips.2 = (bf16[4,2,64,384]{3,2,1,0:T(8,128)(2,1)S(1)}, bf16[4,2,64,384]{3,2,1,0:T(8,128)(2,1)S(1)}) custom-call(s32[1]{0:T(128)} %bitcast.last_ref, bf16[8,8,64,384]{3,2,1,0:T(8,128)(2,1)} %bitcast.11, bf16[8,8,64,384]{3,2,1,0:T(8,128)(2,1)} %bitcast.12, bf16[4,2,64,384]{3,2,1,0:T(8,128)(2,1)} %collective-permute-done.halo_a.halo_b, ...), custom_call_target="tpu_custom_call" | custom-call | flops 7650410496 | bytes 3145728 | tf_op jit(solution)/shard_map/strips/pallas_call | solution.py:192
  130.2 1.2 collective-permute-start.1
  131.4 9.2 %collective-permute-done.1 = bf16[4,2,64,384]{3,2,1,0:T(8,128)(2,1)S(1)} collective-permute-done((bf16[4,2,64,384]{3,2,1,0:T(8,128)(2,1)S(1)}, bf16[4,2,64,384]{3,2,1,0:T(8,128)(2,1)S(1)}, u32[]{:S(2)}, u32[]{:S(2)}) %collective-permute-start.1) | collective-permute-done | bytes 393248 | tf_op jit(solution)/shard_map/ppermute | solution.py:23
  140.7 0.0 collective-permute-done.3
  140.7 2.0 %maximum_maximum_fusion = bf16[8,8,64,384]{3,2,1,0:T(8,128)(2,1)} fusion(bf16[4,1,64,384]{3,2,1,0:T(8,128)(2,1)S(1)} %get-tuple-element.24, bf16[4,6,64,384]{3,2,1,0:T(8,128)(2,1)S(1)} %get-tuple-element.18, bf16[4,1,64,384]{3,2,1,0:T(8,128)(2,1)S(1)} %get-tuple-element.23, bf16[4,1,64,384]{3,2,1,0:T(8,128)(2,1)S(1)} %get-tuple-element.22, ...), kind=kLoop, calls=%fused_computation | loop fusion | flops 7864320 | bytes 6291456 | tf_op jit(solution)/shard_map/concatenate | solution.py:391
  (4 shorter events, 0.1 us)
Async XLA Ops:
  0.0 10.5 %copy-start.7 = (f32[384]{0:T(512)S(1)}, f32[384]{0:T(512)}, u32[]{:S(2)}) copy-start(f32[384]{0:T(512)} %param.10) | copy-start | bytes 4612
  0.0 10.5 %copy-start.8 = (f32[384]{0:T(512)S(1)}, f32[384]{0:T(512)}, u32[]{:S(2)}) copy-start(f32[384]{0:T(512)} %param.11) | copy-start | bytes 4612
  0.0 10.5 %slice-start = ((bf16[384,1152]{1,0:T(8,128)(2,1)}), bf16[384,384]{1,0:T(8,128)(2,1)S(1)}, s32[]{:S(2)}) async-start(bf16[384,1152]{1,0:T(8,128)(2,1)} %wqkv.3), calls=%async_computation | async-start | bytes 589824 | tf_op jit(solution)/shard_map/slice | solution.py:379
  2.5 13.9 %copy-start.1 = (bf16[384,1152]{1,0:T(8,128)(2,1)S(1)}, bf16[384,1152]{1,0:T(8,128)(2,1)}, u32[]{:S(2)}) copy-start(bf16[384,1152]{1,0:T(8,128)(2,1)} %wqkv.3) | copy-start | bytes 2654212
  2.5 13.9 %copy-start.4 = (bf16[384,1152]{1,0:T(8,128)(2,1)S(1)}, bf16[384,1152]{1,0:T(8,128)(2,1)}, u32[]{:S(2)}) copy-start(bf16[384,1152]{1,0:T(8,128)(2,1)} %wc.1) | copy-start | bytes 2654212
  2.5 33.1 %collective-permute-start.2 = (bf16[4,6,64,384]{3,2,1,0:T(8,128)(2,1)}, bf16[4,6,64,384]{3,2,1,0:T(8,128)(2,1)S(1)}, u32[]{:S(2)}, u32[]{:S(2)}) collective-permute-start(bf16[4,6,64,384]{3,2,1,0:T(8,128)(2,1)} %slice.35), channel_id=1, source_target_pairs={{0,15},{1,0},{2,1},{3,2},{4,3},{5,4},{6,5},{7,6},{8,7},{9,8},{10,9... | collective-permute-start | bytes 3538952 | tf_op jit(solution)/shard_map/ppermute | solution.py:23
  9.8 96.5 %collective-permute-start = (bf16[4,2,64,384]{3,2,1,0:T(8,128)(2,1)}, bf16[4,2,64,384]{3,2,1,0:T(8,128)(2,1)}, u32[]{:S(2)}, u32[]{:S(2)}) collective-permute-start(bf16[4,2,64,384]{3,2,1,0:T(8,128)(2,1)} %pad_maximum_fusion), channel_id=1, source_target_pairs={{0,15},{1,0},{2,1},{3,2},{4,3},{5,4},{6,5},{7,6},{8,7},{9,8},{10,9... | collective-permute-start | bytes 1179656 | tf_op jit(solution)/shard_map/ppermute | solution.py:23
  10.7 5.7 %copy-start.5 = (bf16[384,384]{1,0:T(8,128)(2,1)S(1)}, bf16[384,384]{1,0:T(8,128)(2,1)}, u32[]{:S(2)}) copy-start(bf16[384,384]{1,0:T(8,128)(2,1)} %wco.1) | copy-start | bytes 884740
  16.4 1.0 copy-start
  17.4 18.2 %copy-start.6 = (bf16[384,384]{1,0:T(8,128)(2,1)S(1)}, bf16[384,384]{1,0:T(8,128)(2,1)}, u32[]{:S(2)}) copy-start(bf16[384,384]{1,0:T(8,128)(2,1)} %wo.3) | copy-start | bytes 884740
  35.6 70.7 %copy-start.2 = (bf16[384,1536]{1,0:T(8,128)(2,1)S(1)}, bf16[384,1536]{1,0:T(8,128)(2,1)}, u32[]{:S(2)}) copy-start(bf16[384,1536]{1,0:T(8,128)(2,1)} %w1.3) | copy-start | bytes 3538948
  35.6 70.7 %copy-start.3 = (bf16[1536,384]{1,0:T(8,128)(2,1)S(1)}, bf16[1536,384]{1,0:T(8,128)(2,1)}, u32[]{:S(2)}) copy-start(bf16[1536,384]{1,0:T(8,128)(2,1)} %w2.3) | copy-start | bytes 3538948
  106.0 34.7 %collective-permute-start.3 = (bf16[4,6,64,384]{3,2,1,0:T(8,128)(2,1)S(1)}, bf16[4,6,64,384]{3,2,1,0:T(8,128)(2,1)S(1)}, u32[]{:S(2)}, u32[]{:S(2)}) collective-permute-start(bf16[4,6,64,384]{3,2,1,0:T(8,128)(2,1)S(1)} %get-tuple-element.16), channel_id=1, source_target_pairs={{0,1},{1,2},{2,3},{3,4},{4,5},{5,6},{6,7},{7,8},{8,9},{9,10},{10,1... | collective-permute-start | bytes 3538952 | tf_op jit(solution)/shard_map/ppermute | solution.py:23
  130.2 10.5 %collective-permute-start.1 = (bf16[4,2,64,384]{3,2,1,0:T(8,128)(2,1)S(1)}, bf16[4,2,64,384]{3,2,1,0:T(8,128)(2,1)S(1)}, u32[]{:S(2)}, u32[]{:S(2)}) collective-permute-start(bf16[4,2,64,384]{3,2,1,0:T(8,128)(2,1)S(1)} %get-tuple-element.15), channel_id=1, source_target_pairs={{0,1},{1,2},{2,3},{3,4},{4,5},{5,6},{6,7},{7,8},{8,9},{9,10},{10,1... | collective-permute-start | bytes 1179656 | tf_op jit(solution)/shard_map/ppermute | solution.py:23

commit v4 on v2

--- a/solution.py
+++ b/solution.py
@@ -109,7 +109,7 @@
         k4 = qkv_s[1, w, g]
         v4 = qkv_s[2, w, g]
         k_aug = jnp.concatenate([k4, feat_k], axis=1)
-        acc = jnp.zeros((half, 256), jnp.float32)
+        weights, contents = [], []
         peak = jnp.zeros((half, 128), jnp.float32)
         zero = jnp.zeros((), jnp.bfloat16)
         for h in range(4):
@@ -120,8 +120,14 @@
             m = jnp.max(s, axis=1, keepdims=True)
             p = jnp.exp2(s - m).astype(jnp.bfloat16)
             v_aug = jnp.concatenate([v4 * mask, jnp.broadcast_to(mask, (half, 128))], axis=1)
-            acc = acc + jnp.dot(p, v_aug, preferred_element_type=jnp.float32)
+            weights.append(p)
+            contents.append(v_aug)
             peak = jnp.where(mine, m, peak)
+        acc = jnp.dot(
+            jnp.concatenate(weights, axis=1),
+            jnp.concatenate(contents, axis=0),
+            preferred_element_type=jnp.float32,
+        )
         lanes = pl.ds(pl.multiple_of(g * 128, 128), 128)
         kcw = row_of(kc[:, lanes], 2 * strip + w)
         vcw = row_of(vc[:, lanes], 2 * strip + w)
@@ -136,7 +142,7 @@
         att_s[w, g] = att.astype(jnp.bfloat16)
         return carry
 
-    lax.fori_loop(0, 2 * GROUPS, attend, 0)
+    lax.fori_loop(0, 2 * GROUPS, attend, 0, unroll=True)
 
     gain2 = g2[...]
     tile = half // 2
@@ -157,7 +163,7 @@
         y_s[pl.ds(part * (tile // 8), tile // 8), w] = out.reshape(tile // 8, 8, C)
         return carry
 
-    lax.fori_loop(0, 4, finish, 0)
+    lax.fori_loop(0, 4, finish, 0, unroll=True)
     done = pltpu.roll(y_s[...].reshape(rows, C), HALF, 0).astype(jnp.bfloat16)
     done = done.reshape(4, HALF, HALF * 16, C)
     ya = 2 * pl.program_id(0)

time: 138 us -> 113 us (0.82)
  Pallas kernels: 112 us -> 87.2 us
    pallas_call x2, Pallas kernels: 88.8 us -> 64.3 us  [strips_call(): pl.pallas_call(functools.partial(strip_kernel, first, strips), grid=(coun...]
  transfers between devices with their start and end apart: 4 -> 4, of which waited for: 1 -> 1; matrix products, arithmetic and copies ran while one was open for 1% -> 2% of each run, Pallas kernels for 81% -> 78%
where the time goes in v4:
time: 113 us
  Pallas kernels  87.2 us (77%)
  waiting for transfers between devices  9.26 us (8%)
  starting transfers between devices  7.4 us (7%)
  local copies, waits for them, and re-layouts  5.79 us (5%)
  other arithmetic  2.74 us (2%)
    pallas_call x2, Pallas kernels, strips_call(): pl.pallas_call(functools.partial(strip_kernel, first, strips), grid=(coun...  64.3 us
    pallas_call x1, Pallas kernels, carriers(): pl.pallas_call(functools.partial(carrier_kernel, n), out_shape=(shape,) *...  17.2 us
    ppermute x4, waiting for transfers between devices, shifted(): return lax.ppermute(value, axis, pairs)  9.26 us
    ppermute x4, starting transfers between devices, shifted(): return lax.ppermute(value, axis, pairs)  7.4 us
    pallas_call x1, Pallas kernels, half_sums(): pl.pallas_call(sums_kernel, grid=(yh,), out_shape=jax.ShapeDtypeStruct((y...  5.7 us
    slice x1, local copies, waits for them, and re-layouts, body(): sent = volume[:HALF, 2 * lo + 1:2 * hi + 1]  2.45 us
  transfers between devices with their start and end apart: 4, of which 1 were waited for; matrix products, arithmetic and copies ran while one was open for 2% of the time, Pallas kernels for 78%

profile of v4, /device:TPU:0, one launch (start us, length us, event | category | flops | bytes accessed | tf_op | source)
XLA Modules:
  0.0 112.5 jit_solution(8681804682026559619)
XLA Ops:
  0.0 0.0 copy-start.8
  0.0 0.0 copy-start.9
  0.0 2.4 %slice.31 = bf16[4,6,64,384]{3,2,1,0:T(8,128)(2,1)} slice(bf16[8,8,64,384]{3,2,1,0:T(8,128)(2,1)} %bitcast.3), slice={[0:4], [1:7], [0:64], [0:384]} | slice | bytes 2359296 | tf_op jit(solution)/shard_map/slice | solution.py:374
  2.5 0.0 copy-start.3
  2.5 0.0 copy-start.6
  2.5 5.4 %collective-permute-start.2 = (bf16[4,6,64,384]{3,2,1,0:T(8,128)(2,1)}, bf16[4,6,64,384]{3,2,1,0:T(8,128)(2,1)S(1)}, u32[]{:S(2)}, u32[]{:S(2)}) collective-permute-start(bf16[4,6,64,384]{3,2,1,0:T(8,128)(2,1)} %slice.31), channel_id=1, source_target_pairs={{0,15},{1,0},{2,1},{3,2},{4,3},{5,4},{6,5},{7,6},{8,7},{9,8},{10,9... | collective-permute-start | bytes 3538952 | tf_op jit(solution)/shard_map/ppermute | solution.py:23
  7.9 1.1 fusion
  9.0 0.8 pad_maximum_fusion
  9.8 0.7 collective-permute-start
  10.4 0.0 copy-done.8
  10.4 0.0 copy-done.9
  10.4 0.0 copy-start.1
  10.5 5.7 %half_sums.1.parts = f32[8,2,16,384]{3,2,1,0:T(8,128)} custom-call(bf16[8,8,64,384]{3,2,1,0:T(8,128)(2,1)} %bitcast.5), custom_call_target="tpu_custom_call" | custom-call | flops 3145728 | bytes 3145728 | tf_op jit(solution)/shard_map/half_sums/pallas_call | solution.py:235
  16.2 0.0 copy-done.3
  16.2 0.0 copy-done.6
  16.2 0.0 copy-start
  16.2 1.0 copy-done
  17.2 0.0 copy-start.4
  17.2 1.2 %copy-done.4 = bf16[384,1152]{1,0:T(8,128)(2,1)S(1)} copy-done((bf16[384,1152]{1,0:T(8,128)(2,1)S(1)}, bf16[384,1152]{1,0:T(8,128)(2,1)}, u32[]{:S(2)}) %copy-start.4) | copy-done | bytes 884760
  18.3 0.0 copy-start.5
  18.3 0.0 copy-start.7
  18.3 17.2 %carriers.1 = (f32[8,384]{1,0:T(8,128)S(1)}, f32[8,384]{1,0:T(8,128)S(1)}, f32[8,384]{1,0:T(8,128)S(1)}) custom-call(f32[8,2,16,384]{3,2,1,0:T(8,128)S(1)} %copy-done, f32[1,384]{1,0:T(1,128)S(1)} %reshape.20.g1, bf16[384,1152]{1,0:T(8,128)(2,1)S(1)} %copy-done.3, bf16[384,384]{1,0:T(8,128)(2,1)S(1)} %copy-done.6, bf16[384,1152]{1,0:T(8,128)(2,1)S(1)} %copy-done.4), custom_call_target="tpu_custom_call" | custom-call | flops 1000000000 | bytes 30000000 | tf_op jit(solution)/shard_map/carriers/pallas_call | solution.py:339
  35.6 0.0 collective-permute-done.2.halo_a.halo_b
  35.6 0.0 copy-done.1
  35.6 0.0 copy-done.5
  35.6 0.0 copy-done.7
  35.6 0.0 copy-start.2
  35.6 47.6 %strips.3 = (bf16[4,6,64,384]{3,2,1,0:T(8,128)(2,1)S(1)}, bf16[4,6,64,384]{3,2,1,0:T(8,128)(2,1)S(1)}) custom-call(s32[1]{0:T(128)} %bitcast.last_ref, bf16[8,8,64,384]{3,2,1,0:T(8,128)(2,1)} %bitcast.6, bf16[8,8,64,384]{3,2,1,0:T(8,128)(2,1)} %bitcast.7, bf16[4,6,64,384]{3,2,1,0:T(8,128)(2,1)S(1)} %collective-permute-done.2.halo_a.halo_b, ...), custom_call_target="tpu_custom_call" | custom-call | flops 22951231488 | bytes 9437184 | tf_op jit(solution)/shard_map/strips/pallas_call | solution.py:194
  83.3 0.1 collective-permute-start.3
  83.4 0.0 collective-permute-done.halo_a.halo_b
  83.4 0.0 copy-done.2
  83.4 16.7 %strips.2 = (bf16[4,2,64,384]{3,2,1,0:T(8,128)(2,1)S(1)}, bf16[4,2,64,384]{3,2,1,0:T(8,128)(2,1)S(1)}) custom-call(s32[1]{0:T(128)} %bitcast.last_ref, bf16[8,8,64,384]{3,2,1,0:T(8,128)(2,1)} %bitcast.8, bf16[8,8,64,384]{3,2,1,0:T(8,128)(2,1)} %bitcast.9, bf16[4,2,64,384]{3,2,1,0:T(8,128)(2,1)} %collective-permute-done.halo_a.halo_b, ...), custom_call_target="tpu_custom_call" | custom-call | flops 7650410496 | bytes 3145728 | tf_op jit(solution)/shard_map/strips/pallas_call | solution.py:194
  100.1 1.2 %collective-permute-start.1 = (bf16[4,2,64,384]{3,2,1,0:T(8,128)(2,1)S(1)}, bf16[4,2,64,384]{3,2,1,0:T(8,128)(2,1)S(1)}, u32[]{:S(2)}, u32[]{:S(2)}) collective-permute-start(bf16[4,2,64,384]{3,2,1,0:T(8,128)(2,1)S(1)} %get-tuple-element.15), channel_id=1, source_target_pairs={{0,1},{1,2},{2,3},{3,4},{4,5},{5,6},{6,7},{7,8},{8,9},{9,10},{10,1... | collective-permute-start | bytes 1179656 | tf_op jit(solution)/shard_map/ppermute | solution.py:23
  101.3 9.3 %collective-permute-done.1 = bf16[4,2,64,384]{3,2,1,0:T(8,128)(2,1)S(1)} collective-permute-done((bf16[4,2,64,384]{3,2,1,0:T(8,128)(2,1)S(1)}, bf16[4,2,64,384]{3,2,1,0:T(8,128)(2,1)S(1)}, u32[]{:S(2)}, u32[]{:S(2)}) %collective-permute-start.1) | collective-permute-done | bytes 393248 | tf_op jit(solution)/shard_map/ppermute | solution.py:23
  110.6 0.0 collective-permute-done.3
  110.6 1.9 %maximum_maximum_fusion = bf16[8,8,64,384]{3,2,1,0:T(8,128)(2,1)} fusion(bf16[4,1,64,384]{3,2,1,0:T(8,128)(2,1)S(1)} %get-tuple-element.24, bf16[4,6,64,384]{3,2,1,0:T(8,128)(2,1)S(1)} %get-tuple-element.18, bf16[4,1,64,384]{3,2,1,0:T(8,128)(2,1)S(1)} %get-tuple-element.23, bf16[4,1,64,384]{3,2,1,0:T(8,128)(2,1)S(1)} %get-tuple-element.22, ...), kind=kLoop, calls=%fused_computation | loop fusion | flops 7864320 | bytes 6291456 | tf_op jit(solution)/shard_map/concatenate | solution.py:392
  (4 shorter events, 0.1 us)
Async XLA Ops:
  0.0 10.4 %copy-start.8 = (f32[384]{0:T(512)S(1)}, f32[384]{0:T(512)}, u32[]{:S(2)}) copy-start(f32[384]{0:T(512)} %param.10) | copy-start | bytes 4612
  0.0 10.4 %copy-start.9 = (f32[384]{0:T(512)S(1)}, f32[384]{0:T(512)}, u32[]{:S(2)}) copy-start(f32[384]{0:T(512)} %param.11) | copy-start | bytes 4612
  2.5 13.7 %copy-start.3 = (bf16[384,1152]{1,0:T(8,128)(2,1)S(1)}, bf16[384,1152]{1,0:T(8,128)(2,1)}, u32[]{:S(2)}) copy-start(bf16[384,1152]{1,0:T(8,128)(2,1)} %wc.1) | copy-start | bytes 2654212
  2.5 13.7 %copy-start.6 = (bf16[384,384]{1,0:T(8,128)(2,1)S(1)}, bf16[384,384]{1,0:T(8,128)(2,1)}, u32[]{:S(2)}) copy-start(bf16[384,384]{1,0:T(8,128)(2,1)} %wco.1) | copy-start | bytes 884740
  2.5 33.1 %collective-permute-start.2 = (bf16[4,6,64,384]{3,2,1,0:T(8,128)(2,1)}, bf16[4,6,64,384]{3,2,1,0:T(8,128)(2,1)S(1)}, u32[]{:S(2)}, u32[]{:S(2)}) collective-permute-start(bf16[4,6,64,384]{3,2,1,0:T(8,128)(2,1)} %slice.31), channel_id=1, source_target_pairs={{0,15},{1,0},{2,1},{3,2},{4,3},{5,4},{6,5},{7,6},{8,7},{9,8},{10,9... | collective-permute-start | bytes 3538952 | tf_op jit(solution)/shard_map/ppermute | solution.py:23
  9.8 73.6 %collective-permute-start = (bf16[4,2,64,384]{3,2,1,0:T(8,128)(2,1)}, bf16[4,2,64,384]{3,2,1,0:T(8,128)(2,1)}, u32[]{:S(2)}, u32[]{:S(2)}) collective-permute-start(bf16[4,2,64,384]{3,2,1,0:T(8,128)(2,1)} %pad_maximum_fusion), channel_id=1, source_target_pairs={{0,15},{1,0},{2,1},{3,2},{4,3},{5,4},{6,5},{7,6},{8,7},{9,8},{10,9... | collective-permute-start | bytes 1179656 | tf_op jit(solution)/shard_map/ppermute | solution.py:23
  10.4 25.1 %copy-start.1 = (bf16[384,1536]{1,0:T(8,128)(2,1)S(1)}, bf16[384,1536]{1,0:T(8,128)(2,1)}, u32[]{:S(2)}) copy-start(bf16[384,1536]{1,0:T(8,128)(2,1)} %w1.3) | copy-start | bytes 3538948
  16.2 1.0 copy-start
  17.2 1.2 %copy-start.4 = (bf16[384,1152]{1,0:T(8,128)(2,1)S(1)}, bf16[384,1152]{1,0:T(8,128)(2,1)}, u32[]{:S(2)}) copy-start(bf16[384,1152]{1,0:T(8,128)(2,1)} %wqkv.3) | copy-start | bytes 2654212
  18.3 17.2 %copy-start.5 = (bf16[384,1152]{1,0:T(8,128)(2,1)S(1)}, bf16[384,1152]{1,0:T(8,128)(2,1)}, u32[]{:S(2)}) copy-start(bf16[384,1152]{1,0:T(8,128)(2,1)} %wqkv.3) | copy-start | bytes 2654212
  18.3 17.3 %copy-start.7 = (bf16[384,384]{1,0:T(8,128)(2,1)S(1)}, bf16[384,384]{1,0:T(8,128)(2,1)}, u32[]{:S(2)}) copy-start(bf16[384,384]{1,0:T(8,128)(2,1)} %wo.3) | copy-start | bytes 884740
  35.6 47.8 %copy-start.2 = (bf16[1536,384]{1,0:T(8,128)(2,1)S(1)}, bf16[1536,384]{1,0:T(8,128)(2,1)}, u32[]{:S(2)}) copy-start(bf16[1536,384]{1,0:T(8,128)(2,1)} %w2.3) | copy-start | bytes 3538948
  83.3 27.3 %collective-permute-start.3 = (bf16[4,6,64,384]{3,2,1,0:T(8,128)(2,1)S(1)}, bf16[4,6,64,384]{3,2,1,0:T(8,128)(2,1)S(1)}, u32[]{:S(2)}, u32[]{:S(2)}) collective-permute-start(bf16[4,6,64,384]{3,2,1,0:T(8,128)(2,1)S(1)} %get-tuple-element.16), channel_id=1, source_target_pairs={{0,1},{1,2},{2,3},{3,4},{4,5},{5,6},{6,7},{7,8},{8,9},{9,10},{10,1... | collective-permute-start | bytes 3538952 | tf_op jit(solution)/shard_map/ppermute | solution.py:23
  100.1 10.5 %collective-permute-start.1 = (bf16[4,2,64,384]{3,2,1,0:T(8,128)(2,1)S(1)}, bf16[4,2,64,384]{3,2,1,0:T(8,128)(2,1)S(1)}, u32[]{:S(2)}, u32[]{:S(2)}) collective-permute-start(bf16[4,2,64,384]{3,2,1,0:T(8,128)(2,1)S(1)} %get-tuple-element.15), channel_id=1, source_target_pairs={{0,1},{1,2},{2,3},{3,4},{4,5},{5,6},{6,7},{7,8},{8,9},{9,10},{10,1... | collective-permute-start | bytes 1179656 | tf_op jit(solution)/shard_map/ppermute | solution.py:23
